TPU v7x, 128 devices: a whole 4x4x4 slice. The times are simulated.
128 devices in a mesh: ctx: 32 (over y, x, core), head: 4 (over z).
Axes of the slice: x: 4, y: 4, z: 4, core: 2. Of those that a mesh axis runs over, the one named last changes fastest.
Arguments:
- q_lin: float32 [8192, 4096], P('ctx', 'head'), may hold values from -6 to 6
- k_lin: float32 [8192, 4096], P('ctx', 'head'), may hold values from -0.9722718 to 0.9722718
- v_lin: float32 [8192, 4096], P('ctx', 'head'), may hold values from -201 to 201
- log_decay: float32 [32, 8192], P('head', 'ctx'), may hold values from -1 to 0
- lin_gain: float32 [4096], P('head'), may hold values from 0.1 to 1.9
- q_soft: float32 [8192, 6144], P('ctx', 'head'), may hold values from -36 to 36
- k_soft: float32 [8192, 1024], P('ctx', 'head'), may hold values from -4 to 4
- v_soft: float32 [8192, 1024], P('ctx', 'head'), may hold values from -6 to 6
Outputs:
- lin_out: float32 [8192, 4096], P('ctx', 'head')
- soft_out: float32 [8192, 6144], P('ctx', 'head')
All inputs are finite; a program needn't handle non-finite values.
Results may differ from a plain program's by a relative error of at most 0.0003.
Values sent between devices are 32-bit elements; how exact they have to be, the bound alone decides.
A program may use at most 128 MiB of HBM per device.

v0:
```python
import math

import jax
import jax.numpy as jnp
from jax import lax
from jax.sharding import PartitionSpec as P

HD = 128
LH = 32


HIGHEST = lax.Precision.HIGHEST
NEGATIVE = -1e30
EPSILON = 1e-05


def entering(value, axis, combine, identity):
    count, mine = (lax.axis_size(axis), lax.axis_index(axis))
    everything = jax.tree.map(lambda part: lax.all_gather(part, axis), value)
    start = jax.tree.map(
        lambda part, zero: jnp.broadcast_to(jnp.asarray(zero, part.dtype), part.shape),
        value,
        identity,
    )

    def turn(k, before):
        reached = k < mine
        new = combine(before, jax.tree.map(lambda part: part[k], everything))
        return jax.tree.map(lambda a, b: jnp.where(reached, a, b), new, before)

    return lax.fori_loop(0, count, turn, start)


def block_terms(queries, key_rows, value_rows, log_rates):
    length = queries.shape[0]
    cumulative = jnp.cumsum(log_rates, axis=1)
    positions = jnp.arange(length)
    causal = (positions[:, None] >= positions[None, :])[None]
    decay_gaps = cumulative[:, :, None] - cumulative[:, None, :]
    weights = jnp.where(causal, jnp.exp(jnp.where(causal, decay_gaps, 0.0)), 0.0)
    scores = jnp.einsum("thd,shd->hts", queries, key_rows, precision=HIGHEST)
    inside = jnp.einsum("hts,shd->thd", scores * weights, value_rows, precision=HIGHEST)
    block_total = cumulative[:, -1]
    trailing = jnp.exp(block_total[:, None] - cumulative)
    scaled_keys = key_rows * jnp.transpose(trailing)[:, :, None]
    local_state = jnp.einsum("shd,she->hde", scaled_keys, value_rows, precision=HIGHEST)
    leading = jnp.transpose(jnp.exp(cumulative))[:, :, None]
    return (inside, leading, block_total, local_state)


def attend(partial_value, query_rows, query_pos, key_slab, value_slab, key_pos, score_scale):
    old_max, old_total, weighted = partial_value
    scores = jnp.einsum("tkgd,skd->kgts", query_rows, key_slab, precision=HIGHEST) * score_scale
    visible = (key_pos[None, :] <= query_pos[:, None])[None, None]
    scores = jnp.where(visible, scores, NEGATIVE)
    new_max = jnp.maximum(old_max, jnp.max(scores, axis=3))
    weights = jnp.where(visible, jnp.exp(scores - new_max[..., None]), 0.0)
    shrink = jnp.exp(old_max - new_max)
    new_total = old_total * shrink + jnp.sum(weights, axis=3)
    weighted = weighted * shrink[..., None] + jnp.einsum(
        "kgts,skd->kgtd", weights, value_slab, precision=HIGHEST
    )
    return (new_max, new_total, weighted)


def soft_layer(query_sets, k_soft, v_soft, score_scale):
    kv_heads = k_soft.shape[1] // HD
    initial = []
    for query_rows, query_pos in query_sets:
        shape = (query_rows.shape[1], query_rows.shape[2], query_rows.shape[0])
        initial.append(
            (
                jnp.full(shape, NEGATIVE, jnp.float32),
                jnp.zeros(shape, jnp.float32),
                jnp.zeros(shape + (HD,), jnp.float32),
            )
        )
    initial = tuple(initial)
    key_rows = lax.all_gather(k_soft, "ctx", axis=0, tiled=True)
    value_rows = lax.all_gather(v_soft, "ctx", axis=0, tiled=True)
    shard_rows = key_rows.shape[0]
    key_block = math.gcd(shard_rows, 512)
    key_rows = key_rows.reshape(shard_rows // key_block, key_block, kv_heads, HD)
    value_rows = value_rows.reshape(shard_rows // key_block, key_block, kv_heads, HD)

    def visit(block_index, partials):
        key_slab = lax.dynamic_index_in_dim(key_rows, block_index, 0, keepdims=False)
        value_slab = lax.dynamic_index_in_dim(value_rows, block_index, 0, keepdims=False)
        first_key = block_index * key_block
        key_pos = first_key + jnp.arange(key_block)
        updated = []
        for (query_rows, query_pos), partial_value in zip(query_sets, partials):

            def engage(current, query_rows=query_rows, query_pos=query_pos):
                return attend(
                    current, query_rows, query_pos, key_slab, value_slab, key_pos, score_scale
                )

            def remain(current):
                return current

            updated.append(lax.cond(first_key <= jnp.max(query_pos), engage, remain, partial_value))
        return tuple(updated)

    finals = lax.fori_loop(0, shard_rows // key_block, visit, initial)
    results = []
    for final in finals:
        maxima, totals, weighted = final
        merged = weighted / totals[..., None]
        row_count = merged.shape[2]
        results.append(jnp.transpose(merged, (2, 0, 1, 3)).reshape(row_count, -1))
    return results


def body(q_lin, k_lin, v_lin, log_decay, lin_gain, q_soft, k_soft, v_soft):
    row_count = q_lin.shape[0]
    head_count = log_decay.shape[0]
    position = lax.axis_index("ctx")
    queries = q_lin.reshape(row_count, head_count, HD)
    key_rows = k_lin.reshape(row_count, head_count, HD)
    value_rows = v_lin.reshape(row_count, head_count, HD)
    inside, leading, block_total, local_state = block_terms(
        queries, key_rows, value_rows, log_decay
    )

    def chain_step(earlier, later):
        return (earlier[0] + later[0], jnp.exp(later[0])[:, None, None] * earlier[1] + later[1])

    identity = (jnp.zeros_like(block_total), jnp.zeros_like(local_state))
    prefix_pair = entering((block_total, local_state), "ctx", chain_step, identity)
    prior_state = prefix_pair[1]
    linear = inside + leading * jnp.einsum("thd,hde->the", queries, prior_state, precision=HIGHEST)
    linear = linear.reshape(row_count, head_count * HD)
    energy = lax.psum(jnp.sum(linear * linear, axis=1, keepdims=True), "head")
    lin_out = linear * lax.rsqrt(energy / (LH * HD) + EPSILON) * lin_gain
    score_scale = 1.0 / math.sqrt(HD)
    kv_heads = k_soft.shape[1] // HD
    group_size = q_soft.shape[1] // (kv_heads * HD)
    soft_queries = q_soft.reshape(row_count, kv_heads, group_size, HD)
    query_pos = position * row_count + jnp.arange(row_count)
    soft_out = soft_layer([(soft_queries, query_pos)], k_soft, v_soft, score_scale)[0]
    return (lin_out, soft_out)


def solution(mesh):
    return jax.shard_map(
        body,
        mesh=mesh,
        in_specs=(
            P("ctx", "head"),
            P("ctx", "head"),
            P("ctx", "head"),
            P("head", "ctx"),
            P("head"),
            P("ctx", "head"),
            P("ctx", "head"),
            P("ctx", "head"),
        ),
        out_specs=(P("ctx", "head"), P("ctx", "head")),
        check_vma=False,
    )
```

profile of v0, /device:TPU:30, one launch (start us, length us, event | category | flops | bytes accessed | tf_op | source)
XLA Modules:
  0.0 573.1 jit_solution(4927016760311225648)
XLA Ops:
  17.5 59.2 %all-reduce = f32[256]{0:T(256)S(1)} all-reduce(f32[256]{0:T(256)S(1)} %dynamic-update-slice), channel_id=2, replica_groups=mesh['ctx'=32,'head'=4] {'ctx'}, use_global_device_ids=true, to_apply=%add | all-reduce | flops 256 | bytes 2048
  137.9 363.9 %while.33 = (s32[]{:T(128)}, f32[2,6,256]{2,1,0:T(8,128)S(1)}, f32[2,6,256]{2,1,0:T(8,128)S(1)}, f32[2,6,256,128]{3,2,1,0:T(8,128)}, s32[]{:T(128)}, /*index=5*/...) while((s32[]{:T(128)}, f32[2,6,256]{2,1,0:T(8,128)S(1)}, ...), condition=%wide.region_12.13_spmd.clone, body=%wide.region_7.0_spmd.clone.sunk | while | flops 4851637248 | bytes 37959000 | solution.py:105
  138.4 22.2 %conditional.3 = ((f32[2,6,256]{2,1,0:T(8,128)S(1)}, f32[2,6,256]{2,1,0:T(8,128)S(1)}, f32[2,6,256,128]{3,2,1,0:T(8,128)})) conditional(s32[]{:T(128)} %convert_element_type.10, (f32[2,6,256]{2,1,0:T(8,128)S(1)}, f32[2,6,256]{2,1,0:T(8,128)S(1)}, f32[2,6,256,128]{3,2,1,0:T(8,128)}) %tuple.98, (s32[]{:T(128)}, s32[512]{0:T(512)S(1)}, s32[]{:T(128)}, ...), branch_computations={%region_8.8_spmd, %region_9.11_spmd} | conditional | flops 4851637248 | bytes 37955680 | solution.py:102
  147.2 12.2 %multiply_add_fusion = f32[2,6,256,128]{3,2,1,0:T(8,128)S(1)} fusion(f32[2,6,256,128]{3,2,1,0:T(8,128)S(1)} %copy-done.2, f32[2,512,256,6]{2,1,3,0:T(8,128)S(1)} %get-tuple-element.535, f32[2,6,256]{2,1,0:T(8,128)S(1)} %max.6, pred[256,512]{0,1:T(8,128)(4,1)S(1)} %broadcast_compare_fusion, f32[2,6,256]{2,1,0:T(8,128)S(1)} %get-tuple-element.531, ...), kind=kOutput, calls=%fused_computation.11 | convolution fusion | flops 2422996992 | bytes 10117632 | tf_op jit(solution)/shard_map/while/body/eval_jaxpr/cond/branch_1_fun/kgts,skd->kgtd/dot_general | solution.py:60
  161.2 22.2 %conditional.3 = ((f32[2,6,256]{2,1,0:T(8,128)S(1)}, f32[2,6,256]{2,1,0:T(8,128)S(1)}, f32[2,6,256,128]{3,2,1,0:T(8,128)})) conditional(s32[]{:T(128)} %convert_element_type.10, (f32[2,6,256]{2,1,0:T(8,128)S(1)}, f32[2,6,256]{2,1,0:T(8,128)S(1)}, f32[2,6,256,128]{3,2,1,0:T(8,128)}) %tuple.98, (s32[]{:T(128)}, s32[512]{0:T(512)S(1)}, s32[]{:T(128)}, ...), branch_computations={%region_8.8_spmd, %region_9.11_spmd} | conditional | flops 4851637248 | bytes 37955680 | solution.py:102
  170.0 12.2 %multiply_add_fusion = f32[2,6,256,128]{3,2,1,0:T(8,128)S(1)} fusion(f32[2,6,256,128]{3,2,1,0:T(8,128)S(1)} %copy-done.2, f32[2,512,256,6]{2,1,3,0:T(8,128)S(1)} %get-tuple-element.535, f32[2,6,256]{2,1,0:T(8,128)S(1)} %max.6, pred[256,512]{0,1:T(8,128)(4,1)S(1)} %broadcast_compare_fusion, f32[2,6,256]{2,1,0:T(8,128)S(1)} %get-tuple-element.531, ...), kind=kOutput, calls=%fused_computation.11 | convolution fusion | flops 2422996992 | bytes 10117632 | tf_op jit(solution)/shard_map/while/body/eval_jaxpr/cond/branch_1_fun/kgts,skd->kgtd/dot_general | solution.py:60
  183.9 22.2 %conditional.3 = ((f32[2,6,256]{2,1,0:T(8,128)S(1)}, f32[2,6,256]{2,1,0:T(8,128)S(1)}, f32[2,6,256,128]{3,2,1,0:T(8,128)})) conditional(s32[]{:T(128)} %convert_element_type.10, (f32[2,6,256]{2,1,0:T(8,128)S(1)}, f32[2,6,256]{2,1,0:T(8,128)S(1)}, f32[2,6,256,128]{3,2,1,0:T(8,128)}) %tuple.98, (s32[]{:T(128)}, s32[512]{0:T(512)S(1)}, s32[]{:T(128)}, ...), branch_computations={%region_8.8_spmd, %region_9.11_spmd} | conditional | flops 4851637248 | bytes 37955680 | solution.py:102
  192.7 12.2 %multiply_add_fusion = f32[2,6,256,128]{3,2,1,0:T(8,128)S(1)} fusion(f32[2,6,256,128]{3,2,1,0:T(8,128)S(1)} %copy-done.2, f32[2,512,256,6]{2,1,3,0:T(8,128)S(1)} %get-tuple-element.535, f32[2,6,256]{2,1,0:T(8,128)S(1)} %max.6, pred[256,512]{0,1:T(8,128)(4,1)S(1)} %broadcast_compare_fusion, f32[2,6,256]{2,1,0:T(8,128)S(1)} %get-tuple-element.531, ...), kind=kOutput, calls=%fused_computation.11 | convolution fusion | flops 2422996992 | bytes 10117632 | tf_op jit(solution)/shard_map/while/body/eval_jaxpr/cond/branch_1_fun/kgts,skd->kgtd/dot_general | solution.py:60
  206.7 22.2 %conditional.3 = ((f32[2,6,256]{2,1,0:T(8,128)S(1)}, f32[2,6,256]{2,1,0:T(8,128)S(1)}, f32[2,6,256,128]{3,2,1,0:T(8,128)})) conditional(s32[]{:T(128)} %convert_element_type.10, (f32[2,6,256]{2,1,0:T(8,128)S(1)}, f32[2,6,256]{2,1,0:T(8,128)S(1)}, f32[2,6,256,128]{3,2,1,0:T(8,128)}) %tuple.98, (s32[]{:T(128)}, s32[512]{0:T(512)S(1)}, s32[]{:T(128)}, ...), branch_computations={%region_8.8_spmd, %region_9.11_spmd} | conditional | flops 4851637248 | bytes 37955680 | solution.py:102
  215.5 12.2 %multiply_add_fusion = f32[2,6,256,128]{3,2,1,0:T(8,128)S(1)} fusion(f32[2,6,256,128]{3,2,1,0:T(8,128)S(1)} %copy-done.2, f32[2,512,256,6]{2,1,3,0:T(8,128)S(1)} %get-tuple-element.535, f32[2,6,256]{2,1,0:T(8,128)S(1)} %max.6, pred[256,512]{0,1:T(8,128)(4,1)S(1)} %broadcast_compare_fusion, f32[2,6,256]{2,1,0:T(8,128)S(1)} %get-tuple-element.531, ...), kind=kOutput, calls=%fused_computation.11 | convolution fusion | flops 2422996992 | bytes 10117632 | tf_op jit(solution)/shard_map/while/body/eval_jaxpr/cond/branch_1_fun/kgts,skd->kgtd/dot_general | solution.py:60
  229.4 22.2 %conditional.3 = ((f32[2,6,256]{2,1,0:T(8,128)S(1)}, f32[2,6,256]{2,1,0:T(8,128)S(1)}, f32[2,6,256,128]{3,2,1,0:T(8,128)})) conditional(s32[]{:T(128)} %convert_element_type.10, (f32[2,6,256]{2,1,0:T(8,128)S(1)}, f32[2,6,256]{2,1,0:T(8,128)S(1)}, f32[2,6,256,128]{3,2,1,0:T(8,128)}) %tuple.98, (s32[]{:T(128)}, s32[512]{0:T(512)S(1)}, s32[]{:T(128)}, ...), branch_computations={%region_8.8_spmd, %region_9.11_spmd} | conditional | flops 4851637248 | bytes 37955680 | solution.py:102
  238.2 12.2 %multiply_add_fusion = f32[2,6,256,128]{3,2,1,0:T(8,128)S(1)} fusion(f32[2,6,256,128]{3,2,1,0:T(8,128)S(1)} %copy-done.2, f32[2,512,256,6]{2,1,3,0:T(8,128)S(1)} %get-tuple-element.535, f32[2,6,256]{2,1,0:T(8,128)S(1)} %max.6, pred[256,512]{0,1:T(8,128)(4,1)S(1)} %broadcast_compare_fusion, f32[2,6,256]{2,1,0:T(8,128)S(1)} %get-tuple-element.531, ...), kind=kOutput, calls=%fused_computation.11 | convolution fusion | flops 2422996992 | bytes 10117632 | tf_op jit(solution)/shard_map/while/body/eval_jaxpr/cond/branch_1_fun/kgts,skd->kgtd/dot_general | solution.py:60
  252.2 22.2 %conditional.3 = ((f32[2,6,256]{2,1,0:T(8,128)S(1)}, f32[2,6,256]{2,1,0:T(8,128)S(1)}, f32[2,6,256,128]{3,2,1,0:T(8,128)})) conditional(s32[]{:T(128)} %convert_element_type.10, (f32[2,6,256]{2,1,0:T(8,128)S(1)}, f32[2,6,256]{2,1,0:T(8,128)S(1)}, f32[2,6,256,128]{3,2,1,0:T(8,128)}) %tuple.98, (s32[]{:T(128)}, s32[512]{0:T(512)S(1)}, s32[]{:T(128)}, ...), branch_computations={%region_8.8_spmd, %region_9.11_spmd} | conditional | flops 4851637248 | bytes 37955680 | solution.py:102
  261.0 12.2 %multiply_add_fusion = f32[2,6,256,128]{3,2,1,0:T(8,128)S(1)} fusion(f32[2,6,256,128]{3,2,1,0:T(8,128)S(1)} %copy-done.2, f32[2,512,256,6]{2,1,3,0:T(8,128)S(1)} %get-tuple-element.535, f32[2,6,256]{2,1,0:T(8,128)S(1)} %max.6, pred[256,512]{0,1:T(8,128)(4,1)S(1)} %broadcast_compare_fusion, f32[2,6,256]{2,1,0:T(8,128)S(1)} %get-tuple-element.531, ...), kind=kOutput, calls=%fused_computation.11 | convolution fusion | flops 2422996992 | bytes 10117632 | tf_op jit(solution)/shard_map/while/body/eval_jaxpr/cond/branch_1_fun/kgts,skd->kgtd/dot_general | solution.py:60
  274.9 22.2 %conditional.3 = ((f32[2,6,256]{2,1,0:T(8,128)S(1)}, f32[2,6,256]{2,1,0:T(8,128)S(1)}, f32[2,6,256,128]{3,2,1,0:T(8,128)})) conditional(s32[]{:T(128)} %convert_element_type.10, (f32[2,6,256]{2,1,0:T(8,128)S(1)}, f32[2,6,256]{2,1,0:T(8,128)S(1)}, f32[2,6,256,128]{3,2,1,0:T(8,128)}) %tuple.98, (s32[]{:T(128)}, s32[512]{0:T(512)S(1)}, s32[]{:T(128)}, ...), branch_computations={%region_8.8_spmd, %region_9.11_spmd} | conditional | flops 4851637248 | bytes 37955680 | solution.py:102
  283.7 12.2 %multiply_add_fusion = f32[2,6,256,128]{3,2,1,0:T(8,128)S(1)} fusion(f32[2,6,256,128]{3,2,1,0:T(8,128)S(1)} %copy-done.2, f32[2,512,256,6]{2,1,3,0:T(8,128)S(1)} %get-tuple-element.535, f32[2,6,256]{2,1,0:T(8,128)S(1)} %max.6, pred[256,512]{0,1:T(8,128)(4,1)S(1)} %broadcast_compare_fusion, f32[2,6,256]{2,1,0:T(8,128)S(1)} %get-tuple-element.531, ...), kind=kOutput, calls=%fused_computation.11 | convolution fusion | flops 2422996992 | bytes 10117632 | tf_op jit(solution)/shard_map/while/body/eval_jaxpr/cond/branch_1_fun/kgts,skd->kgtd/dot_general | solution.py:60
  297.6 22.2 %conditional.3 = ((f32[2,6,256]{2,1,0:T(8,128)S(1)}, f32[2,6,256]{2,1,0:T(8,128)S(1)}, f32[2,6,256,128]{3,2,1,0:T(8,128)})) conditional(s32[]{:T(128)} %convert_element_type.10, (f32[2,6,256]{2,1,0:T(8,128)S(1)}, f32[2,6,256]{2,1,0:T(8,128)S(1)}, f32[2,6,256,128]{3,2,1,0:T(8,128)}) %tuple.98, (s32[]{:T(128)}, s32[512]{0:T(512)S(1)}, s32[]{:T(128)}, ...), branch_computations={%region_8.8_spmd, %region_9.11_spmd} | conditional | flops 4851637248 | bytes 37955680 | solution.py:102
  306.4 12.2 %multiply_add_fusion = f32[2,6,256,128]{3,2,1,0:T(8,128)S(1)} fusion(f32[2,6,256,128]{3,2,1,0:T(8,128)S(1)} %copy-done.2, f32[2,512,256,6]{2,1,3,0:T(8,128)S(1)} %get-tuple-element.535, f32[2,6,256]{2,1,0:T(8,128)S(1)} %max.6, pred[256,512]{0,1:T(8,128)(4,1)S(1)} %broadcast_compare_fusion, f32[2,6,256]{2,1,0:T(8,128)S(1)} %get-tuple-element.531, ...), kind=kOutput, calls=%fused_computation.11 | convolution fusion | flops 2422996992 | bytes 10117632 | tf_op jit(solution)/shard_map/while/body/eval_jaxpr/cond/branch_1_fun/kgts,skd->kgtd/dot_general | solution.py:60
  320.4 22.2 %conditional.3 = ((f32[2,6,256]{2,1,0:T(8,128)S(1)}, f32[2,6,256]{2,1,0:T(8,128)S(1)}, f32[2,6,256,128]{3,2,1,0:T(8,128)})) conditional(s32[]{:T(128)} %convert_element_type.10, (f32[2,6,256]{2,1,0:T(8,128)S(1)}, f32[2,6,256]{2,1,0:T(8,128)S(1)}, f32[2,6,256,128]{3,2,1,0:T(8,128)}) %tuple.98, (s32[]{:T(128)}, s32[512]{0:T(512)S(1)}, s32[]{:T(128)}, ...), branch_computations={%region_8.8_spmd, %region_9.11_spmd} | conditional | flops 4851637248 | bytes 37955680 | solution.py:102
  329.2 12.2 %multiply_add_fusion = f32[2,6,256,128]{3,2,1,0:T(8,128)S(1)} fusion(f32[2,6,256,128]{3,2,1,0:T(8,128)S(1)} %copy-done.2, f32[2,512,256,6]{2,1,3,0:T(8,128)S(1)} %get-tuple-element.535, f32[2,6,256]{2,1,0:T(8,128)S(1)} %max.6, pred[256,512]{0,1:T(8,128)(4,1)S(1)} %broadcast_compare_fusion, f32[2,6,256]{2,1,0:T(8,128)S(1)} %get-tuple-element.531, ...), kind=kOutput, calls=%fused_computation.11 | convolution fusion | flops 2422996992 | bytes 10117632 | tf_op jit(solution)/shard_map/while/body/eval_jaxpr/cond/branch_1_fun/kgts,skd->kgtd/dot_general | solution.py:60
  343.1 22.2 %conditional.3 = ((f32[2,6,256]{2,1,0:T(8,128)S(1)}, f32[2,6,256]{2,1,0:T(8,128)S(1)}, f32[2,6,256,128]{3,2,1,0:T(8,128)})) conditional(s32[]{:T(128)} %convert_element_type.10, (f32[2,6,256]{2,1,0:T(8,128)S(1)}, f32[2,6,256]{2,1,0:T(8,128)S(1)}, f32[2,6,256,128]{3,2,1,0:T(8,128)}) %tuple.98, (s32[]{:T(128)}, s32[512]{0:T(512)S(1)}, s32[]{:T(128)}, ...), branch_computations={%region_8.8_spmd, %region_9.11_spmd} | conditional | flops 4851637248 | bytes 37955680 | solution.py:102
  351.9 12.2 %multiply_add_fusion = f32[2,6,256,128]{3,2,1,0:T(8,128)S(1)} fusion(f32[2,6,256,128]{3,2,1,0:T(8,128)S(1)} %copy-done.2, f32[2,512,256,6]{2,1,3,0:T(8,128)S(1)} %get-tuple-element.535, f32[2,6,256]{2,1,0:T(8,128)S(1)} %max.6, pred[256,512]{0,1:T(8,128)(4,1)S(1)} %broadcast_compare_fusion, f32[2,6,256]{2,1,0:T(8,128)S(1)} %get-tuple-element.531, ...), kind=kOutput, calls=%fused_computation.11 | convolution fusion | flops 2422996992 | bytes 10117632 | tf_op jit(solution)/shard_map/while/body/eval_jaxpr/cond/branch_1_fun/kgts,skd->kgtd/dot_general | solution.py:60
  365.9 22.2 %conditional.3 = ((f32[2,6,256]{2,1,0:T(8,128)S(1)}, f32[2,6,256]{2,1,0:T(8,128)S(1)}, f32[2,6,256,128]{3,2,1,0:T(8,128)})) conditional(s32[]{:T(128)} %convert_element_type.10, (f32[2,6,256]{2,1,0:T(8,128)S(1)}, f32[2,6,256]{2,1,0:T(8,128)S(1)}, f32[2,6,256,128]{3,2,1,0:T(8,128)}) %tuple.98, (s32[]{:T(128)}, s32[512]{0:T(512)S(1)}, s32[]{:T(128)}, ...), branch_computations={%region_8.8_spmd, %region_9.11_spmd} | conditional | flops 4851637248 | bytes 37955680 | solution.py:102
  374.7 12.2 %multiply_add_fusion = f32[2,6,256,128]{3,2,1,0:T(8,128)S(1)} fusion(f32[2,6,256,128]{3,2,1,0:T(8,128)S(1)} %copy-done.2, f32[2,512,256,6]{2,1,3,0:T(8,128)S(1)} %get-tuple-element.535, f32[2,6,256]{2,1,0:T(8,128)S(1)} %max.6, pred[256,512]{0,1:T(8,128)(4,1)S(1)} %broadcast_compare_fusion, f32[2,6,256]{2,1,0:T(8,128)S(1)} %get-tuple-element.531, ...), kind=kOutput, calls=%fused_computation.11 | convolution fusion | flops 2422996992 | bytes 10117632 | tf_op jit(solution)/shard_map/while/body/eval_jaxpr/cond/branch_1_fun/kgts,skd->kgtd/dot_general | solution.py:60
  388.6 22.2 %conditional.3 = ((f32[2,6,256]{2,1,0:T(8,128)S(1)}, f32[2,6,256]{2,1,0:T(8,128)S(1)}, f32[2,6,256,128]{3,2,1,0:T(8,128)})) conditional(s32[]{:T(128)} %convert_element_type.10, (f32[2,6,256]{2,1,0:T(8,128)S(1)}, f32[2,6,256]{2,1,0:T(8,128)S(1)}, f32[2,6,256,128]{3,2,1,0:T(8,128)}) %tuple.98, (s32[]{:T(128)}, s32[512]{0:T(512)S(1)}, s32[]{:T(128)}, ...), branch_computations={%region_8.8_spmd, %region_9.11_spmd} | conditional | flops 4851637248 | bytes 37955680 | solution.py:102
  397.4 12.2 %multiply_add_fusion = f32[2,6,256,128]{3,2,1,0:T(8,128)S(1)} fusion(f32[2,6,256,128]{3,2,1,0:T(8,128)S(1)} %copy-done.2, f32[2,512,256,6]{2,1,3,0:T(8,128)S(1)} %get-tuple-element.535, f32[2,6,256]{2,1,0:T(8,128)S(1)} %max.6, pred[256,512]{0,1:T(8,128)(4,1)S(1)} %broadcast_compare_fusion, f32[2,6,256]{2,1,0:T(8,128)S(1)} %get-tuple-element.531, ...), kind=kOutput, calls=%fused_computation.11 | convolution fusion | flops 2422996992 | bytes 10117632 | tf_op jit(solution)/shard_map/while/body/eval_jaxpr/cond/branch_1_fun/kgts,skd->kgtd/dot_general | solution.py:60
  411.3 22.2 %conditional.3 = ((f32[2,6,256]{2,1,0:T(8,128)S(1)}, f32[2,6,256]{2,1,0:T(8,128)S(1)}, f32[2,6,256,128]{3,2,1,0:T(8,128)})) conditional(s32[]{:T(128)} %convert_element_type.10, (f32[2,6,256]{2,1,0:T(8,128)S(1)}, f32[2,6,256]{2,1,0:T(8,128)S(1)}, f32[2,6,256,128]{3,2,1,0:T(8,128)}) %tuple.98, (s32[]{:T(128)}, s32[512]{0:T(512)S(1)}, s32[]{:T(128)}, ...), branch_computations={%region_8.8_spmd, %region_9.11_spmd} | conditional | flops 4851637248 | bytes 37955680 | solution.py:102
  420.1 12.2 %multiply_add_fusion = f32[2,6,256,128]{3,2,1,0:T(8,128)S(1)} fusion(f32[2,6,256,128]{3,2,1,0:T(8,128)S(1)} %copy-done.2, f32[2,512,256,6]{2,1,3,0:T(8,128)S(1)} %get-tuple-element.535, f32[2,6,256]{2,1,0:T(8,128)S(1)} %max.6, pred[256,512]{0,1:T(8,128)(4,1)S(1)} %broadcast_compare_fusion, f32[2,6,256]{2,1,0:T(8,128)S(1)} %get-tuple-element.531, ...), kind=kOutput, calls=%fused_computation.11 | convolution fusion | flops 2422996992 | bytes 10117632 | tf_op jit(solution)/shard_map/while/body/eval_jaxpr/cond/branch_1_fun/kgts,skd->kgtd/dot_general | solution.py:60
  434.1 22.2 %conditional.3 = ((f32[2,6,256]{2,1,0:T(8,128)S(1)}, f32[2,6,256]{2,1,0:T(8,128)S(1)}, f32[2,6,256,128]{3,2,1,0:T(8,128)})) conditional(s32[]{:T(128)} %convert_element_type.10, (f32[2,6,256]{2,1,0:T(8,128)S(1)}, f32[2,6,256]{2,1,0:T(8,128)S(1)}, f32[2,6,256,128]{3,2,1,0:T(8,128)}) %tuple.98, (s32[]{:T(128)}, s32[512]{0:T(512)S(1)}, s32[]{:T(128)}, ...), branch_computations={%region_8.8_spmd, %region_9.11_spmd} | conditional | flops 4851637248 | bytes 37955680 | solution.py:102
  456.8 22.2 %conditional.3 = ((f32[2,6,256]{2,1,0:T(8,128)S(1)}, f32[2,6,256]{2,1,0:T(8,128)S(1)}, f32[2,6,256,128]{3,2,1,0:T(8,128)})) conditional(s32[]{:T(128)} %convert_element_type.10, (f32[2,6,256]{2,1,0:T(8,128)S(1)}, f32[2,6,256]{2,1,0:T(8,128)S(1)}, f32[2,6,256,128]{3,2,1,0:T(8,128)}) %tuple.98, (s32[]{:T(128)}, s32[512]{0:T(512)S(1)}, s32[]{:T(128)}, ...), branch_computations={%region_8.8_spmd, %region_9.11_spmd} | conditional | flops 4851637248 | bytes 37955680 | solution.py:102
  479.6 22.2 %conditional.3 = ((f32[2,6,256]{2,1,0:T(8,128)S(1)}, f32[2,6,256]{2,1,0:T(8,128)S(1)}, f32[2,6,256,128]{3,2,1,0:T(8,128)})) conditional(s32[]{:T(128)} %convert_element_type.10, (f32[2,6,256]{2,1,0:T(8,128)S(1)}, f32[2,6,256]{2,1,0:T(8,128)S(1)}, f32[2,6,256,128]{3,2,1,0:T(8,128)}) %tuple.98, (s32[]{:T(128)}, s32[512]{0:T(512)S(1)}, s32[]{:T(128)}, ...), branch_computations={%region_8.8_spmd, %region_9.11_spmd} | conditional | flops 4851637248 | bytes 37955680 | solution.py:102
  508.1 38.9 %while.34 = (s32[]{:T(128)}, f32[8,128,128]{2,1,0:T(8,128)S(1)}, s32[]{:T(128)}, f32[32,8]{1,0:T(8,128)S(1)}, f32[32,8,128,128]{3,2,1,0:T(8,128)}, /*index=5*/s32[]{:T(128)}, s32[]{:T(128)}) while((s32[]{:T(128)}, f32[8,128,128]{2,1,0:T(8,128)S(1)}, s32[]{:T(128)}, f32[32,8]{1,0:T(8,128)S(1)}, f32[32,8,128,128]{3,2,1,0:T(8,128)}, ...), condition=%wide.region_3.4_spmd.clone, body=%wide.region_2.3_spmd.clone.sunk | while | flops 524292 | bytes 1573065 | solution.py:31
  (343 shorter events, 328.8 us)
Async XLA Ops:
  7.2 75.3 %copy-start = (f32[256,1024]{1,0:T(8,128)S(1)}, f32[256,1024]{1,0:T(8,128)}, u32[]{:S(2)}) copy-start(f32[256,1024]{1,0:T(8,128)} %param.14) | copy-start | bytes 3145732
  7.2 79.7 %all-gather.6.cloned.1.call-start = ((), (), s32[]{:S(2)}) async-start(), calls=%async_computation | async-start | bytes 8650752 | tf_op jit(solution)/shard_map/all_gather | solution.py:79
  7.9 110.0 %all-gather.8.cloned.1.call-start = ((), (), s32[]{:S(2)}) async-start(), calls=%async_computation.1 | async-start | bytes 8650752 | tf_op jit(solution)/shard_map/all_gather | solution.py:80
  8.7 499.4 %all-gather.10.cloned.1.call-start = ((), (), s32[]{:S(2)}) async-start(), calls=%async_computation.2 | async-start | bytes 17301504 | tf_op jit(solution)/shard_map/all_gather | solution.py:19
  11.7 3.6 copy-start.1
  138.6 8.6 %copy-start.2 = (f32[2,6,256,128]{3,2,1,0:T(8,128)S(1)}, f32[2,6,256,128]{3,2,1,0:T(8,128)}, u32[]{:S(2)}) copy-start(f32[2,6,256,128]{3,2,1,0:T(8,128)} %get-tuple-element.401) | copy-start | bytes 4718596 | tf_op jit(solution)/shard_map/while/body/eval_jaxpr/cond
  159.5 1.1 copy-start.3
  161.4 8.6 %copy-start.2 = (f32[2,6,256,128]{3,2,1,0:T(8,128)S(1)}, f32[2,6,256,128]{3,2,1,0:T(8,128)}, u32[]{:S(2)}) copy-start(f32[2,6,256,128]{3,2,1,0:T(8,128)} %get-tuple-element.401) | copy-start | bytes 4718596 | tf_op jit(solution)/shard_map/while/body/eval_jaxpr/cond
  182.2 1.1 copy-start.3
  184.1 8.6 %copy-start.2 = (f32[2,6,256,128]{3,2,1,0:T(8,128)S(1)}, f32[2,6,256,128]{3,2,1,0:T(8,128)}, u32[]{:S(2)}) copy-start(f32[2,6,256,128]{3,2,1,0:T(8,128)} %get-tuple-element.401) | copy-start | bytes 4718596 | tf_op jit(solution)/shard_map/while/body/eval_jaxpr/cond
  205.0 1.1 copy-start.3
  206.9 8.6 %copy-start.2 = (f32[2,6,256,128]{3,2,1,0:T(8,128)S(1)}, f32[2,6,256,128]{3,2,1,0:T(8,128)}, u32[]{:S(2)}) copy-start(f32[2,6,256,128]{3,2,1,0:T(8,128)} %get-tuple-element.401) | copy-start | bytes 4718596 | tf_op jit(solution)/shard_map/while/body/eval_jaxpr/cond
  227.7 1.1 copy-start.3
  229.6 8.6 %copy-start.2 = (f32[2,6,256,128]{3,2,1,0:T(8,128)S(1)}, f32[2,6,256,128]{3,2,1,0:T(8,128)}, u32[]{:S(2)}) copy-start(f32[2,6,256,128]{3,2,1,0:T(8,128)} %get-tuple-element.401) | copy-start | bytes 4718596 | tf_op jit(solution)/shard_map/while/body/eval_jaxpr/cond
  250.4 1.1 copy-start.3
  252.4 8.6 %copy-start.2 = (f32[2,6,256,128]{3,2,1,0:T(8,128)S(1)}, f32[2,6,256,128]{3,2,1,0:T(8,128)}, u32[]{:S(2)}) copy-start(f32[2,6,256,128]{3,2,1,0:T(8,128)} %get-tuple-element.401) | copy-start | bytes 4718596 | tf_op jit(solution)/shard_map/while/body/eval_jaxpr/cond
  273.2 1.1 copy-start.3
  275.1 8.6 %copy-start.2 = (f32[2,6,256,128]{3,2,1,0:T(8,128)S(1)}, f32[2,6,256,128]{3,2,1,0:T(8,128)}, u32[]{:S(2)}) copy-start(f32[2,6,256,128]{3,2,1,0:T(8,128)} %get-tuple-element.401) | copy-start | bytes 4718596 | tf_op jit(solution)/shard_map/while/body/eval_jaxpr/cond
  297.8 8.6 %copy-start.2 = (f32[2,6,256,128]{3,2,1,0:T(8,128)S(1)}, f32[2,6,256,128]{3,2,1,0:T(8,128)}, u32[]{:S(2)}) copy-start(f32[2,6,256,128]{3,2,1,0:T(8,128)} %get-tuple-element.401) | copy-start | bytes 4718596 | tf_op jit(solution)/shard_map/while/body/eval_jaxpr/cond
  318.7 1.1 copy-start.3
  320.6 8.6 %copy-start.2 = (f32[2,6,256,128]{3,2,1,0:T(8,128)S(1)}, f32[2,6,256,128]{3,2,1,0:T(8,128)}, u32[]{:S(2)}) copy-start(f32[2,6,256,128]{3,2,1,0:T(8,128)} %get-tuple-element.401) | copy-start | bytes 4718596 | tf_op jit(solution)/shard_map/while/body/eval_jaxpr/cond
  343.3 8.6 %copy-start.2 = (f32[2,6,256,128]{3,2,1,0:T(8,128)S(1)}, f32[2,6,256,128]{3,2,1,0:T(8,128)}, u32[]{:S(2)}) copy-start(f32[2,6,256,128]{3,2,1,0:T(8,128)} %get-tuple-element.401) | copy-start | bytes 4718596 | tf_op jit(solution)/shard_map/while/body/eval_jaxpr/cond
  366.1 8.6 %copy-start.2 = (f32[2,6,256,128]{3,2,1,0:T(8,128)S(1)}, f32[2,6,256,128]{3,2,1,0:T(8,128)}, u32[]{:S(2)}) copy-start(f32[2,6,256,128]{3,2,1,0:T(8,128)} %get-tuple-element.401) | copy-start | bytes 4718596 | tf_op jit(solution)/shard_map/while/body/eval_jaxpr/cond
  388.8 8.6 %copy-start.2 = (f32[2,6,256,128]{3,2,1,0:T(8,128)S(1)}, f32[2,6,256,128]{3,2,1,0:T(8,128)}, u32[]{:S(2)}) copy-start(f32[2,6,256,128]{3,2,1,0:T(8,128)} %get-tuple-element.401) | copy-start | bytes 4718596 | tf_op jit(solution)/shard_map/while/body/eval_jaxpr/cond
  411.5 8.6 %copy-start.2 = (f32[2,6,256,128]{3,2,1,0:T(8,128)S(1)}, f32[2,6,256,128]{3,2,1,0:T(8,128)}, u32[]{:S(2)}) copy-start(f32[2,6,256,128]{3,2,1,0:T(8,128)} %get-tuple-element.401) | copy-start | bytes 4718596 | tf_op jit(solution)/shard_map/while/body/eval_jaxpr/cond
  432.4 1.1 copy-start.3
  434.3 8.6 %copy-start.2 = (f32[2,6,256,128]{3,2,1,0:T(8,128)S(1)}, f32[2,6,256,128]{3,2,1,0:T(8,128)}, u32[]{:S(2)}) copy-start(f32[2,6,256,128]{3,2,1,0:T(8,128)} %get-tuple-element.401) | copy-start | bytes 4718596 | tf_op jit(solution)/shard_map/while/body/eval_jaxpr/cond
  457.0 8.6 %copy-start.2 = (f32[2,6,256,128]{3,2,1,0:T(8,128)S(1)}, f32[2,6,256,128]{3,2,1,0:T(8,128)}, u32[]{:S(2)}) copy-start(f32[2,6,256,128]{3,2,1,0:T(8,128)} %get-tuple-element.401) | copy-start | bytes 4718596 | tf_op jit(solution)/shard_map/while/body/eval_jaxpr/cond
  479.8 8.6 %copy-start.2 = (f32[2,6,256,128]{3,2,1,0:T(8,128)S(1)}, f32[2,6,256,128]{3,2,1,0:T(8,128)}, u32[]{:S(2)}) copy-start(f32[2,6,256,128]{3,2,1,0:T(8,128)} %get-tuple-element.401) | copy-start | bytes 4718596 | tf_op jit(solution)/shard_map/while/body/eval_jaxpr/cond
  500.6 1.1 copy-start.3
  505.0 43.1 %copy-start.4 = (f32[256,1024]{1,0:T(8,128)S(1)}, f32[256,1024]{1,0:T(8,128)}, u32[]{:S(2)}) copy-start(f32[256,1024]{1,0:T(8,128)} %param.16) | copy-start | bytes 3145732
  546.9 18.5 %copy-start.5 = (f32[1024]{0:T(1024)S(1)}, f32[1024]{0:T(1024)}, u32[]{:S(2)}) copy-start(f32[1024]{0:T(1024)} %param.18) | copy-start | bytes 12292
  (7 other events, 8.0 us)
Sparse Core Ops, SparseCore 0:
  10.3 52.9 all-gather.5
  65.5 52.3 all-gather.7
  120.2 71.9 all-gather.9
where the time goes:
time: 577 us; the launch traced here: 573 us
  matrix products  322 us (56%)
  local copies, waits for them, and re-layouts  72.5 us (13%)
  blocking collectives  69.9 us (12%)
  other arithmetic  68.9 us (12%)
  between operations  14.5 us (3%)
  waiting for transfers between devices  13.6 us (2%)
  loops' own time  11.8 us (2%)
    dot_general x16, matrix products, attend(): jnp.einsum('kgts,skd->kgtd', weights, value_slab, precision=HIGHEST)  195 us
    dot_general x16, matrix products, attend(): jnp.einsum('tkgd,skd->kgts', query_rows, key_slab, precision=HIGHEST)  113 us
    unnamed x1, blocking collectives  59.2 us
    select_n x32, other arithmetic, turn(): return jax.tree.map(lambda a, b: jnp.where(reached, a, b), new, before)  37.5 us
    unnamed x16, local copies, waits for them, and re-layouts  25.6 us
    reduce_sum x16, other arithmetic, attend(): new_total = old_total * shrink + jnp.sum(weights, axis=3)  24 us
    cond x80, local copies, waits for them, and re-layouts  18.2 us
    all_gather x1, waiting for transfers between devices, soft_layer(): value_rows = lax.all_gather(v_soft, 'ctx', axis=0, tiled=True)  12.2 us
  transfers between devices with their start and end apart: 3, of which 1 were waited for; matrix products, arithmetic and copies ran while one was open for 69% of the time, Pallas kernels for 0%

commit v1 on v0

v1 whole, which is shorter than its diff:
```python
import functools
import math

import jax
import jax.numpy as jnp
from jax import lax
from jax.experimental import pallas as pl
from jax.experimental.pallas import tpu as pltpu
from jax.sharding import PartitionSpec as P

HD = 128
LH = 32
EPSILON = 1e-05
NEGATIVE = -1e30
F32 = jnp.float32
BF16 = jnp.bfloat16
NT = (((1,), (1,)), ((), ()))
TN = (((0,), (0,)), ((), ()))
ROWS = 256
KEYS = 512
GROUP = 6
TILES = GROUP * ROWS
NEAR = ((0, 0), (2, 0), (0, 3), (0, 1), (2, 3), (2, 1), (0, 2), (2, 2))


def halves(value):
    high = value.astype(BF16)
    return high, (value - high.astype(F32)).astype(BF16)


def dot3(left, right, dims):
    (la,), (ra,) = dims[0]
    lh, ll = halves(left)
    rh, rl = halves(right)
    return lax.dot_general(
        jnp.concatenate([lh, ll, lh], la),
        jnp.concatenate([rh, rh, rl], ra),
        dims,
        preferred_element_type=F32,
    )


def kernel(
    q_lin, k_lin, v_lin, log_decay, gain, q_soft, k_soft, v_soft,
    lin_out, soft_out,
    kv, kv_out, q_in, q3, k3, v2, m_all, l_all, acc, o_send,
    local, gathered, prior, entering, energy, energy_in, cum_row, cum_col,
    swap_send, swap_recv, send, recv, o_ss, o_rs, l_ss, l_rs, e_ss, e_rs, n_ss, n_rs,
):
    me = lax.axis_index("ctx")
    z = lax.axis_index("head")
    core, x, y = lax.rem(me, 2), lax.rem(me // 2, 4), me // 8
    half = y // 2
    other = 1 - half

    def device(yy, xx, cc):
        return (yy * 4 + xx) * 2 + cc

    y_pair = y + 1 - 2 * lax.rem(y, 2)
    ys = (y, 3 - y, y_pair, 3 - y_pair)
    right, left = lax.rem(x + 1, 4), lax.rem(x + 3, 4)
    partner = device(3 - y, x, core)
    targets = (device(y, right, core), device(y, left, core), device(y, x, 1 - core), device(y_pair, x, core))

    def remote(src, dst, ss, rs, ctx):
        return pltpu.make_async_remote_copy(
            src_ref=src, dst_ref=dst, send_sem=ss, recv_sem=rs, device_id={"ctx": ctx, "head": z}
        )

    barrier = pltpu.get_barrier_semaphore()

    @pl.loop(1, 32)
    def _(j):
        pl.semaphore_signal(barrier, inc=1, device_id={"ctx": lax.rem(me + j, 32), "head": z})

    for j in range(1, 4):
        pl.semaphore_signal(barrier, inc=1, device_id={"ctx": me, "head": lax.rem(z + j, 4)})
    mine_col = pl.multiple_of(half * HD, HD)
    other_col = pl.multiple_of(other * HD, HD)
    kv[0, core, 0] = k_soft[:, pl.ds(mine_col, HD)]
    kv[0, core, 1] = v_soft[:, pl.ds(mine_col, HD)]
    kv_out[0] = k_soft[:, pl.ds(other_col, HD)]
    kv_out[1] = v_soft[:, pl.ds(other_col, HD)]
    pl.semaphore_wait(barrier, 34)

    def hop(a, dx, kind):
        slot = 4 * a + dx
        if kind == 2:
            return remote(kv.at[slot, core], kv.at[slot, core], send.at[slot, 2], recv.at[slot, 2], targets[2])
        if kind == 3:
            to = 4 * (a + 2)
            return remote(kv.at[slot, core], kv.at[to, core], send.at[slot, 3], recv.at[to, 0], targets[3])
        if dx == 0:
            to = 4 * a + (3, 1)[kind]
            return remote(kv.at[slot, core], kv.at[to, core], send.at[slot, kind], recv.at[to, 0], targets[kind])
        to = 4 * a + 2
        part = pl.ds(128 * kind, 128)
        return remote(
            kv.at[slot, core, :, part], kv.at[to, core, :, part], send.at[slot, kind], recv.at[to, kind], targets[kind]
        )

    def kinds(a, dx):
        if dx == 0:
            return (3, 0, 1, 2) if a < 2 else (0, 1, 2)
        return {3: (0, 2), 1: (1, 2), 2: (2,)}[dx]

    swap_kv = remote(kv_out, kv.at[4, core], swap_send.at[0], swap_recv.at[0], partner)
    q_cols = pl.ds(pl.multiple_of(other * GROUP * HD, HD), GROUP * HD)
    swap_q = remote(q_soft.at[:, q_cols], q_in, swap_send.at[1], swap_recv.at[1], partner)

    def arrive(a, dx):
        slot = 4 * a + dx
        if (a, dx) == (1, 0):
            swap_kv.wait_recv()
        elif dx == 2:
            for kind in (0, 1):
                part = kv.at[slot, core, :, pl.ds(128 * kind, 128)]
                remote(part, part, send.at[slot, kind], recv.at[slot, kind], targets[2]).wait_recv()
        elif (a, dx) != (0, 0):
            part = kv.at[slot, core]
            remote(part, part, send.at[slot, 0], recv.at[slot, 0], targets[2]).wait_recv()
        for kind in kinds(a, dx):
            hop(a, dx, kind).start()

    arrive(0, 0)

    @pl.when(half == 0)
    def _():
        swap_kv.start()
        swap_q.start()

    @pl.when(half == 1)
    def _():
        swap_q.start()
        swap_kv.start()

    scale = math.log2(math.e) / math.sqrt(HD)

    def take_queries(g, ref, first):
        for r in range(GROUP):
            col = first + r * HD
            if not isinstance(col, int):
                col = pl.multiple_of(col, HD)
            high, low = halves(ref[:, pl.ds(col, HD)] * scale)
            rows = slice(r * ROWS, (r + 1) * ROWS)
            q3[g, rows, :HD] = high
            q3[g, rows, HD : 2 * HD] = high
            q3[g, rows, 2 * HD :] = low

    m_all[...] = jnp.full_like(m_all, NEGATIVE)
    l_all[...] = jnp.zeros_like(l_all)
    acc[...] = jnp.zeros_like(acc)

    rates = log_decay[...]
    s_at = lax.broadcasted_iota(jnp.int32, (ROWS, ROWS), 0)
    t_at = lax.broadcasted_iota(jnp.int32, (ROWS, ROWS), 1)
    cum_row[...] = jnp.dot(
        rates, jnp.where(s_at <= t_at, 1.0, 0.0), precision=lax.Precision.HIGHEST, preferred_element_type=F32
    )
    cum_col[...] = cum_row[...].T

    def lightning_head(hd):
        cols = slice(hd * HD, (hd + 1) * HD)
        q, k, v = q_lin[:, cols], k_lin[:, cols], v_lin[:, cols]
        down = cum_col[:, hd : hd + 1]
        gaps = jnp.where(t_at <= s_at, down - cum_row[hd : hd + 1, :], NEGATIVE)
        scores = dot3(q, k, NT)
        lin_out[:, cols] = dot3(scores * jnp.exp(gaps), v, (((1,), (0,)), ((), ())))
        total = cum_col[ROWS - 1 : ROWS, hd : hd + 1]
        state = dot3(k * jnp.exp(total - down), v, TN)
        for part in range(4):
            local[hd * 4 + part, :32] = state[part * 32 : (part + 1) * 32]
            local[hd * 4 + part, 32:] = jnp.broadcast_to(jnp.exp(total), (8, HD))

    for hd in range(4):
        lightning_head(hd)
    arrive(2, 0)
    for hd in range(4, 8):
        lightning_head(hd)

    def slice_out(j):
        to = lax.rem(me + j, 32)
        return remote(local.at[to], gathered.at[me], l_ss.at[j], l_rs.at[j], to)

    def slice_in(j):
        come = lax.rem(me + 32 - j, 32)
        return remote(local.at[me], gathered.at[come], l_ss.at[j], l_rs.at[j], come)

    @pl.loop(1, 32)
    def _(j):
        slice_out(j).start()

    gathered[me] = local[me]
    take_queries(0, q_soft, half * GROUP * HD)

    def prior_out(j):
        to = lax.rem(me + j, 32)
        return remote(prior.at[to], entering.at[me], e_ss.at[j], e_rs.at[j], to)

    def prior_in(j):
        come = lax.rem(me + 32 - j, 32)
        return remote(prior.at[me], entering.at[come], e_ss.at[j], e_rs.at[j], come)

    def combine():
        @pl.loop(1, 32)
        def _(j):
            slice_in(j).wait_recv()

        def turn(i, before):
            prior[i] = before
            return before * gathered[i, 32:33, :] + gathered[i, :32]

        lax.fori_loop(0, 32, turn, jnp.zeros((32, HD), F32))

        @pl.loop(1, 32)
        def _(j):
            prior_out(j).start()

        entering[me] = prior[me]

    def energy_out(j):
        return pltpu.make_async_remote_copy(
            src_ref=energy,
            dst_ref=energy_in.at[j - 1],
            send_sem=n_ss.at[j - 1],
            recv_sem=n_rs.at[j - 1],
            device_id={"ctx": me, "head": lax.rem(z + j, 4)},
        )

    def add_prior():
        @pl.loop(1, 32)
        def _(j):
            prior_in(j).wait_recv()

        sums = jnp.zeros((ROWS, HD), F32)
        for hd in range(8):
            cols = slice(hd * HD, (hd + 1) * HD)
            state = jnp.concatenate([entering[hd * 4 + part] for part in range(4)], 0)
            reach = dot3(q_lin[:, cols], state, (((1,), (0,)), ((), ())))
            linear = lin_out[:, cols] + jnp.exp(cum_col[:, hd : hd + 1]) * reach
            lin_out[:, cols] = linear
            sums = sums + linear * linear
        energy[...] = sums
        for j in range(1, 4):
            energy_out(j).start()

    def normalize():
        sums = energy[...]
        for j in range(1, 4):
            energy_out(j).wait_recv()
            sums = sums + energy_in[j - 1]
        total = jnp.sum(sums, axis=1, keepdims=True)
        ratio = jnp.broadcast_to(lax.rsqrt(total / (LH * HD) + EPSILON), (ROWS, HD))
        for hd in range(8):
            cols = slice(hd * HD, (hd + 1) * HD)
            lin_out[:, cols] = lin_out[:, cols] * ratio * gain[:, cols]

    def prepare(slot):
        part = kv.at[slot, 1 - core]
        remote(part, part, send.at[slot, 2], recv.at[slot, 2], targets[2]).wait_recv()
        for c in range(2):
            rows = slice(c * ROWS, (c + 1) * ROWS)
            high, low = halves(kv[slot, c, 0])
            k3[slot, rows, :HD] = high
            k3[slot, rows, HD : 2 * HD] = low
            k3[slot, rows, 2 * HD :] = high
            high, low = halves(kv[slot, c, 1])
            for copy in range(2):
                rows = slice(copy * KEYS + c * ROWS, copy * KEYS + (c + 1) * ROWS)
                v2[slot, rows, :HD] = high
                v2[slot, rows, HD:] = low

    def tile(g, slot, r, masked):
        rows = slice(r * ROWS, (r + 1) * ROWS)
        scores = lax.dot_general(q3[g, rows, :], k3[slot], NT, preferred_element_type=F32)
        if masked:
            at = lax.broadcasted_iota(jnp.int32, (ROWS, KEYS), 0) + core * ROWS
            key = lax.broadcasted_iota(jnp.int32, (ROWS, KEYS), 1)
            scores = jnp.where(key <= at, scores, NEGATIVE)
        before = m_all[g, rows, :]
        after = jnp.maximum(before, jnp.max(scores, axis=1, keepdims=True))
        weights = jnp.exp2(scores - jnp.concatenate([after] * (KEYS // HD), 1))
        shrink = jnp.exp2(before - after)
        sums = weights[:, :HD]
        for j in range(1, KEYS // HD):
            sums = sums + weights[:, j * HD : (j + 1) * HD]
        l_all[g, rows, :] = l_all[g, rows, :] * shrink + sums
        high, low = halves(weights)
        summed = jnp.dot(jnp.concatenate([high, low], 1), v2[slot], preferred_element_type=F32)
        acc[g, rows, :] = acc[g, rows, :] * jnp.concatenate([shrink, shrink], 1) + summed
        m_all[g, rows, :] = after

    def result(g, r):
        rows = slice(r * ROWS, (r + 1) * ROWS)
        total = jnp.sum(l_all[g, rows, :], axis=1, keepdims=True)
        return (acc[g, rows, :HD] + acc[g, rows, HD:]) / total

    def o_out(r, col):
        cols = pl.ds(pl.multiple_of(col * GROUP * HD + r * HD, HD), HD)
        return remote(o_send.at[r], soft_out.at[:, cols], o_ss.at[r], o_rs.at[r], partner)

    events = {
        0: lambda: (arrive(0, 3), arrive(0, 1)),
        1: lambda: (arrive(2, 3), arrive(2, 1), combine()),
        2: lambda: arrive(0, 2),
        3: lambda: arrive(2, 2),
        4: lambda: arrive(1, 0),
        5: lambda: arrive(3, 0),
        8: lambda: (swap_q.wait_recv(), take_queries(1, q_in, 0), add_prior()),
        9: lambda: (arrive(1, 3), arrive(1, 1)),
        10: lambda: (arrive(3, 3), arrive(3, 1)),
        12: lambda: arrive(1, 2),
        13: lambda: arrive(3, 2),
        14: normalize,
    }
    mine_at, partner_at = y * 4 + x, (3 - y) * 4 + x

    def pick(k, values):
        out = values[0]
        for at in range(1, 8):
            out = jnp.where(k == at, values[at], out)
        return out

    @pl.loop(0, 32)
    def _(t):
        for at, act in events.items():

            @pl.when(t == at)
            def _(act=act):
                act()

        k = lax.rem(t, 8)
        far = t // 16
        g = jnp.where((t >= 8) & (t < 24), 1, 0)
        a = pick(k, [p[0] for p in NEAR]) + far
        dx = pick(k, [p[1] for p in NEAR])
        slot = 4 * a + dx
        row = jnp.where(a == 0, ys[0], jnp.where(a == 1, ys[1], jnp.where(a == 2, ys[2], ys[3])))
        keys_at = row * 4 + lax.rem(x + dx, 4)
        asks = jnp.where(g == 0, mine_at, partner_at)

        @pl.when((t < 8) | ((t >= 16) & (t < 24)))
        def _():
            prepare(slot)

        @pl.when(keys_at < asks)
        def _():
            for r in range(GROUP):
                tile(g, slot, r, False)

        @pl.when(keys_at == asks)
        def _():
            for r in range(GROUP):
                tile(g, slot, r, True)

        @pl.when(t == 23)
        def _():
            for r in range(GROUP):
                o_send[r] = result(1, r)
                o_out(r, half).start()

    for r in range(GROUP):
        cols = pl.ds(pl.multiple_of(half * GROUP * HD + r * HD, HD), HD)
        soft_out[:, cols] = result(0, r)
    for r in range(GROUP):
        o_out(r, other).wait_recv()

    swap_kv.wait_send()
    swap_q.wait_send()
    for a in range(4):
        for dx in range(4):
            for kind in kinds(a, dx):
                hop(a, dx, kind).wait_send()
    for r in range(GROUP):
        o_out(r, half).wait_send()
    for j in range(1, 4):
        energy_out(j).wait_send()

    @pl.loop(1, 32)
    def _(j):
        slice_out(j).wait_send()
        prior_out(j).wait_send()


def body(q_lin, k_lin, v_lin, log_decay, lin_gain, q_soft, k_soft, v_soft):
    vmem = pl.BlockSpec(memory_space=pltpu.VMEM)
    dma = pltpu.SemaphoreType.DMA
    return pl.pallas_call(
        kernel,
        out_shape=(
            jax.ShapeDtypeStruct(q_lin.shape, F32),
            jax.ShapeDtypeStruct(q_soft.shape, F32),
        ),
        in_specs=[vmem] * 8,
        out_specs=(vmem, vmem),
        scratch_shapes=[
            pltpu.VMEM((16, 2, 2, ROWS, HD), F32),
            pltpu.VMEM((2, ROWS, HD), F32),
            pltpu.VMEM((ROWS, GROUP * HD), F32),
            pltpu.VMEM((2, TILES, 3 * HD), BF16),
            pltpu.VMEM((16, KEYS, 3 * HD), BF16),
            pltpu.VMEM((16, 2 * KEYS, 2 * HD), BF16),
            pltpu.VMEM((2, TILES, HD), F32),
            pltpu.VMEM((2, TILES, HD), F32),
            pltpu.VMEM((2, TILES, 2 * HD), F32),
            pltpu.VMEM((GROUP, ROWS, HD), F32),
            pltpu.VMEM((32, 40, HD), F32),
            pltpu.VMEM((32, 40, HD), F32),
            pltpu.VMEM((32, 32, HD), F32),
            pltpu.VMEM((32, 32, HD), F32),
            pltpu.VMEM((ROWS, HD), F32),
            pltpu.VMEM((3, ROWS, HD), F32),
            pltpu.VMEM((8, ROWS), F32),
            pltpu.VMEM((ROWS, 8), F32),
            dma((2,)), dma((2,)), dma((16, 4)), dma((16, 3)), dma((GROUP,)), dma((GROUP,)),
            dma((32,)), dma((32,)), dma((32,)), dma((32,)), dma((3,)), dma((3,)),
        ],
        compiler_params=pltpu.CompilerParams(
            collective_id=0, has_side_effects=True, vmem_limit_bytes=60 << 20
        ),
        cost_estimate=pl.CostEstimate(
            flops=34 * 4 * TILES * ROWS * HD, bytes_accessed=12 << 20, transcendentals=34 * TILES * ROWS
        ),
        name="attention",
    )(q_lin, k_lin, v_lin, log_decay, lin_gain.reshape(1, -1), q_soft, k_soft, v_soft)


def solution(mesh):
    return jax.shard_map(
        body,
        mesh=mesh,
        in_specs=(
            P("ctx", "head"),
            P("ctx", "head"),
            P("ctx", "head"),
            P("head", "ctx"),
            P("head"),
            P("ctx", "head"),
            P("ctx", "head"),
            P("ctx", "head"),
        ),
        out_specs=(P("ctx", "head"), P("ctx", "head")),
        check_vma=False,
    )
```

time: 577 us -> 124 us (0.21)
  matrix products: 322 us -> 0 us
  Pallas kernels: 0 us -> 120 us
  blocking collectives: 69.9 us -> 0 us
  local copies, waits for them, and re-layouts: 72.5 us -> 3.57 us
  other arithmetic: 68.9 us -> 0 us
  between operations: 14.5 us -> 0.65 us
  waiting for transfers between devices: 13.6 us -> 0 us
  loops' own time: 11.8 us -> 0 us
    dot_general x36 -> x0, matrix products: 322 us -> none  [the longest x16 195 us: attend(): jnp.einsum('kgts,skd->kgtd', weights, value_slab, precision=HIGHEST)]
    pallas_call x0 -> x1, Pallas kernels: none -> 120 us  [body(): pl.pallas_call(kernel, out_shape=(jax.ShapeDtypeStruct(q_lin.shape, F32),...]
    unnamed x1 -> x0, blocking collectives: 59.2 us -> none
    select_n x32 -> x0, other arithmetic: 37.5 us -> none  [turn(): return jax.tree.map(lambda a, b: jnp.where(reached, a, b), new, before)]
    reshape x4 -> x0, local copies, waits for them, and re-layouts: 24.6 us -> none  [the longest x1 10.8 us: soft_layer(): key_rows.reshape(shard_rows // key_block, key_block, kv_heads, HD)]
    reduce_sum x16 -> x0, other arithmetic: 24 us -> none  [attend(): new_total = old_total * shrink + jnp.sum(weights, axis=3)]
    unnamed x16 -> x4, local copies, waits for them, and re-layouts: 25.6 us -> 3.57 us
    cond x80 -> x0, local copies, waits for them, and re-layouts: 18.2 us -> none
  transfers between devices with their start and end apart: 3 -> 0, of which waited for: 1 -> 0; matrix products, arithmetic and copies ran while one was open for 69% -> 0% of each run, Pallas kernels for 0% -> 0%
where the time goes in v1:
time: 124 us
  Pallas kernels  120 us (97%)
  local copies, waits for them, and re-layouts  3.57 us (3%)
    pallas_call x1, Pallas kernels, body(): pl.pallas_call(kernel, out_shape=(jax.ShapeDtypeStruct(q_lin.shape, F32),...  120 us
    unnamed x4, local copies, waits for them, and re-layouts  3.57 us

profile of v1, /device:TPU:30, one launch (start us, length us, event | category | flops | bytes accessed | tf_op | source)
XLA Modules:
  0.0 124.2 jit_solution(3338498071625800796)
XLA Ops:
  0.6 120.0 %attention.1 = (f32[256,1024]{1,0:T(8,128)}, f32[256,1536]{1,0:T(8,128)}) custom-call(f32[256,1024]{1,0:T(8,128)} %q_lin.1, f32[256,1024]{1,0:T(8,128)} %k_lin.1, f32[256,1024]{1,0:T(8,128)} %v_lin.1, f32[8,256]{1,0:T(8,128)} %log_decay.1, f32[1,1024]{1,0:T(1,128)} %bitcast.1, f32[256,1536]{1,0:T(8,128)} %q_soft.1, f32[256,256]{1,0:T(8,128)} %k_soft.1, ...), custom_call_target="tpu_custom_call" | custom-call | flops 6845104128 | bytes 12582912 | tf_op jit(solution)/shard_map/attention/pallas_call | solution.py:388
  120.6 0.0 copy-start
  120.6 2.4 %copy.12 = f32[256,1024]{1,0:T(8,128)} copy(f32[256,1024]{1,0:T(8,128)} %get-tuple-element.4) | data formatting | bytes 2097152
  123.1 0.0 copy-done
  123.1 1.1 copy.13
Async XLA Ops:
  120.6 2.4 %copy-start = (f32[256,1536]{1,0:T(8,128)S(1)}, f32[256,1536]{1,0:T(8,128)}, u32[]{:S(2)}) copy-start(f32[256,1536]{1,0:T(8,128)} %get-tuple-element.5) | copy-start | bytes 4718596

commit v2 on v1

--- a/solution.py
+++ b/solution.py
@@ -20,7 +20,9 @@
 KEYS = 512
 GROUP = 6
 TILES = GROUP * ROWS
-NEAR = ((0, 0), (2, 0), (0, 3), (0, 1), (2, 3), (2, 1), (0, 2), (2, 2))
+COLUMNS = (0, 3, 1, 2)
+LOW = ((0, 0, 1), (1, 0, 0), (0, 2, 1), (1, 2, 0), (1, 1, 1), (1, 3, 1))
+HIGH = ((0, 0, 1), (0, 1, 1), (1, 1, 0), (1, 3, 1), (0, 3, 0), (0, 2, 1))
 
 
 def halves(value):
@@ -44,14 +46,17 @@
     q_lin, k_lin, v_lin, log_decay, gain, q_soft, k_soft, v_soft,
     lin_out, soft_out,
     kv, kv_out, q_in, q3, k3, v2, m_all, l_all, acc, o_send,
-    local, gathered, prior, entering, energy, energy_in, cum_row, cum_col,
-    swap_send, swap_recv, send, recv, o_ss, o_rs, l_ss, l_rs, e_ss, e_rs, n_ss, n_rs,
+    local, gathered, prior, reach_decay, row_out, row_in, entering, energy, energy_in, cum_row, cum_col,
+    swap_send, swap_recv, send, recv, o_ss, o_rs, l_ss, l_rs, r_ss, r_rs, e_ss, e_rs, n_ss, n_rs,
 ):
     me = lax.axis_index("ctx")
     z = lax.axis_index("head")
     core, x, y = lax.rem(me, 2), lax.rem(me // 2, 4), me // 8
     half = y // 2
     other = 1 - half
+    low, high_half = half == 0, half == 1
+    inner = (y == 1) | (y == 2)
+    always = y >= 0
 
     def device(yy, xx, cc):
         return (yy * 4 + xx) * 2 + cc
@@ -60,7 +65,14 @@
     ys = (y, 3 - y, y_pair, 3 - y_pair)
     right, left = lax.rem(x + 1, 4), lax.rem(x + 3, 4)
     partner = device(3 - y, x, core)
-    targets = (device(y, right, core), device(y, left, core), device(y, x, 1 - core), device(y_pair, x, core))
+    across = lax.rem(x + 2, 4)
+    targets = (
+        device(y, right, core),
+        device(y, left, core),
+        device(y, x, 1 - core),
+        device(y_pair, x, core),
+        device(y, across, core),
+    )
 
     def remote(src, dst, ss, rs, ctx):
         return pltpu.make_async_remote_copy(
@@ -69,9 +81,16 @@
 
     barrier = pltpu.get_barrier_semaphore()
 
-    @pl.loop(1, 32)
+    at_row = lax.rem(me, 8)
+    row_start = me - at_row
+
+    @pl.loop(1, 8)
     def _(j):
-        pl.semaphore_signal(barrier, inc=1, device_id={"ctx": lax.rem(me + j, 32), "head": z})
+        pl.semaphore_signal(barrier, inc=1, device_id={"ctx": row_start + lax.rem(at_row + j, 8), "head": z})
+
+    @pl.loop(1, 4)
+    def _(j):
+        pl.semaphore_signal(barrier, inc=1, device_id={"ctx": device(lax.rem(y + j, 4), x, core), "head": z})
 
     for j in range(1, 4):
         pl.semaphore_signal(barrier, inc=1, device_id={"ctx": me, "head": lax.rem(z + j, 4)})
@@ -81,46 +100,52 @@
     kv[0, core, 1] = v_soft[:, pl.ds(mine_col, HD)]
     kv_out[0] = k_soft[:, pl.ds(other_col, HD)]
     kv_out[1] = v_soft[:, pl.ds(other_col, HD)]
-    pl.semaphore_wait(barrier, 34)
+    pl.semaphore_wait(barrier, 13)
 
     def hop(a, dx, kind):
         slot = 4 * a + dx
-        if kind == 2:
-            return remote(kv.at[slot, core], kv.at[slot, core], send.at[slot, 2], recv.at[slot, 2], targets[2])
-        if kind == 3:
-            to = 4 * (a + 2)
-            return remote(kv.at[slot, core], kv.at[to, core], send.at[slot, 3], recv.at[to, 0], targets[3])
+        to = {0: 4 * a + 3, 1: 4 * a + 1, 4: 4 * a + 2, 2: slot, 3: slot + 8}[kind]
+        return remote(
+            kv.at[slot, core], kv.at[to, core], send.at[slot, kind], recv.at[to, int(kind == 2)], targets[kind]
+        )
+
+    def present(a):
+        return (always, always, jnp.logical_not(inner & high_half), jnp.logical_not(inner & low))[a]
+
+    def onward(a, dx):
+        out = []
+        if a < 2:
+            out.append((inner | (low, high_half)[a] if dx == 0 else inner, 3))
+            if a == 1 and dx != 0:
+                out = []
         if dx == 0:
-            to = 4 * a + (3, 1)[kind]
-            return remote(kv.at[slot, core], kv.at[to, core], send.at[slot, kind], recv.at[to, 0], targets[kind])
-        to = 4 * a + 2
-        part = pl.ds(128 * kind, 128)
-        return remote(
-            kv.at[slot, core, :, part], kv.at[to, core, :, part], send.at[slot, kind], recv.at[to, kind], targets[kind]
-        )
-
-    def kinds(a, dx):
-        if dx == 0:
-            return (3, 0, 1, 2) if a < 2 else (0, 1, 2)
-        return {3: (0, 2), 1: (1, 2), 2: (2,)}[dx]
+            when = (always, always, inner & low, present(3))[a]
+            out += [(when, 0), (when, 1), (when, 4)]
+        return out + [(present(a), 2)]
 
     swap_kv = remote(kv_out, kv.at[4, core], swap_send.at[0], swap_recv.at[0], partner)
     q_cols = pl.ds(pl.multiple_of(other * GROUP * HD, HD), GROUP * HD)
     swap_q = remote(q_soft.at[:, q_cols], q_in, swap_send.at[1], swap_recv.at[1], partner)
 
+    def guarded(when, act):
+        if when is always:
+            act()
+        else:
+            pl.when(when)(act)
+
     def arrive(a, dx):
         slot = 4 * a + dx
+
+        def wait():
+            part = kv.at[slot, core]
+            remote(part, part, send.at[slot, 0], recv.at[slot, 0], targets[2]).wait_recv()
+
         if (a, dx) == (1, 0):
             swap_kv.wait_recv()
-        elif dx == 2:
-            for kind in (0, 1):
-                part = kv.at[slot, core, :, pl.ds(128 * kind, 128)]
-                remote(part, part, send.at[slot, kind], recv.at[slot, kind], targets[2]).wait_recv()
         elif (a, dx) != (0, 0):
-            part = kv.at[slot, core]
-            remote(part, part, send.at[slot, 0], recv.at[slot, 0], targets[2]).wait_recv()
-        for kind in kinds(a, dx):
-            hop(a, dx, kind).start()
+            guarded(present(a), wait)
+        for when, kind in onward(a, dx):
+            guarded(when, lambda kind=kind: hop(a, dx, kind).start())
 
     arrive(0, 0)
 
@@ -168,55 +193,78 @@
         lin_out[:, cols] = dot3(scores * jnp.exp(gaps), v, (((1,), (0,)), ((), ())))
         total = cum_col[ROWS - 1 : ROWS, hd : hd + 1]
         state = dot3(k * jnp.exp(total - down), v, TN)
-        for part in range(4):
-            local[hd * 4 + part, :32] = state[part * 32 : (part + 1) * 32]
-            local[hd * 4 + part, 32:] = jnp.broadcast_to(jnp.exp(total), (8, HD))
-
-    for hd in range(4):
+        local[hd, :HD] = state
+        local[hd, HD:] = jnp.broadcast_to(jnp.exp(total), (8, HD))
+
+    for hd in range(8):
         lightning_head(hd)
-    arrive(2, 0)
-    for hd in range(4, 8):
-        lightning_head(hd)
 
     def slice_out(j):
-        to = lax.rem(me + j, 32)
-        return remote(local.at[to], gathered.at[me], l_ss.at[j], l_rs.at[j], to)
+        to = lax.rem(at_row + j, 8)
+        return remote(local.at[to], gathered.at[at_row], l_ss.at[j], l_rs.at[j], row_start + to)
 
     def slice_in(j):
-        come = lax.rem(me + 32 - j, 32)
-        return remote(local.at[me], gathered.at[come], l_ss.at[j], l_rs.at[j], come)
-
-    @pl.loop(1, 32)
+        come = lax.rem(at_row + 8 - j, 8)
+        return remote(local.at[at_row], gathered.at[come], l_ss.at[j], l_rs.at[j], row_start + come)
+
+    @pl.loop(1, 8)
     def _(j):
         slice_out(j).start()
 
-    gathered[me] = local[me]
+    gathered[at_row] = local[at_row]
     take_queries(0, q_soft, half * GROUP * HD)
 
-    def prior_out(j):
-        to = lax.rem(me + j, 32)
-        return remote(prior.at[to], entering.at[me], e_ss.at[j], e_rs.at[j], to)
-
-    def prior_in(j):
-        come = lax.rem(me + 32 - j, 32)
-        return remote(prior.at[me], entering.at[come], e_ss.at[j], e_rs.at[j], come)
-
-    def combine():
-        @pl.loop(1, 32)
+    def total_out(j):
+        return remote(row_out, row_in.at[y], r_ss.at[j], r_rs.at[j], device(lax.rem(y + j, 4), x, core))
+
+    def total_in(j):
+        come = lax.rem(y + 4 - j, 4)
+        return remote(row_out, row_in.at[come], r_ss.at[j], r_rs.at[j], device(come, x, core))
+
+    def combine_row():
+        @pl.loop(1, 8)
         def _(j):
             slice_in(j).wait_recv()
 
-        def turn(i, before):
-            prior[i] = before
-            return before * gathered[i, 32:33, :] + gathered[i, :32]
-
-        lax.fori_loop(0, 32, turn, jnp.zeros((32, HD), F32))
-
-        @pl.loop(1, 32)
+        decay = jnp.ones((8, HD), F32)
+        state = jnp.zeros((HD, HD), F32)
+        for i in range(8):
+            prior[i] = state
+            reach_decay[i] = decay
+            state = state * gathered[i, HD : HD + 1, :] + gathered[i, :HD]
+            decay = decay * gathered[i, HD:, :]
+        row_out[:HD] = state
+        row_out[HD:] = decay
+
+        @pl.loop(1, 4)
+        def _(j):
+            total_out(j).start()
+
+    def prior_out(j):
+        to = lax.rem(at_row + j, 8)
+        return remote(prior.at[to], entering.at[at_row], e_ss.at[j], e_rs.at[j], row_start + to)
+
+    def prior_in(j):
+        come = lax.rem(at_row + 8 - j, 8)
+        return remote(prior.at[at_row], entering.at[come], e_ss.at[j], e_rs.at[j], row_start + come)
+
+    def combine():
+        @pl.loop(1, 4)
+        def _(j):
+            total_in(j).wait_recv()
+
+        row_in[y] = row_out[...]
+        state = jnp.zeros((HD, HD), F32)
+        for i in range(3):
+            state = jnp.where(i < y, state * row_in[i, HD : HD + 1, :] + row_in[i, :HD], state)
+        for i in range(8):
+            prior[i] = prior[i] + reach_decay[i, :1, :] * state
+
+        @pl.loop(1, 8)
         def _(j):
             prior_out(j).start()
 
-        entering[me] = prior[me]
+        entering[at_row] = prior[at_row]
 
     def energy_out(j):
         return pltpu.make_async_remote_copy(
@@ -228,15 +276,14 @@
         )
 
     def add_prior():
-        @pl.loop(1, 32)
+        @pl.loop(1, 8)
         def _(j):
             prior_in(j).wait_recv()
 
         sums = jnp.zeros((ROWS, HD), F32)
         for hd in range(8):
             cols = slice(hd * HD, (hd + 1) * HD)
-            state = jnp.concatenate([entering[hd * 4 + part] for part in range(4)], 0)
-            reach = dot3(q_lin[:, cols], state, (((1,), (0,)), ((), ())))
+            reach = dot3(q_lin[:, cols], entering[hd], (((1,), (0,)), ((), ())))
             linear = lin_out[:, cols] + jnp.exp(cum_col[:, hd : hd + 1]) * reach
             lin_out[:, cols] = linear
             sums = sums + linear * linear
@@ -257,7 +304,7 @@
 
     def prepare(slot):
         part = kv.at[slot, 1 - core]
-        remote(part, part, send.at[slot, 2], recv.at[slot, 2], targets[2]).wait_recv()
+        remote(part, part, send.at[slot, 2], recv.at[slot, 1], targets[2]).wait_recv()
         for c in range(2):
             rows = slice(c * ROWS, (c + 1) * ROWS)
             high, low = halves(kv[slot, c, 0])
@@ -299,47 +346,61 @@
         cols = pl.ds(pl.multiple_of(col * GROUP * HD + r * HD, HD), HD)
         return remote(o_send.at[r], soft_out.at[:, cols], o_ss.at[r], o_rs.at[r], partner)
 
-    events = {
-        0: lambda: (arrive(0, 3), arrive(0, 1)),
-        1: lambda: (arrive(2, 3), arrive(2, 1), combine()),
-        2: lambda: arrive(0, 2),
-        3: lambda: arrive(2, 2),
-        4: lambda: arrive(1, 0),
-        5: lambda: arrive(3, 0),
-        8: lambda: (swap_q.wait_recv(), take_queries(1, q_in, 0), add_prior()),
-        9: lambda: (arrive(1, 3), arrive(1, 1)),
-        10: lambda: (arrive(3, 3), arrive(3, 1)),
-        12: lambda: arrive(1, 2),
-        13: lambda: arrive(3, 2),
-        14: normalize,
-    }
+    def take_partner():
+        swap_q.wait_recv()
+        take_queries(1, q_in, 0)
+
+    def give_back():
+        for r in range(GROUP):
+            o_send[r] = result(1, r)
+            o_out(r, half).start()
+
+    def column(a):
+        for dx in (3, 1, 2):
+            arrive(a, dx)
+
+    events = (
+        (0, 10, lambda: arrive(2, 0)),
+        (6, 0, lambda: arrive(1, 0)),
+        (1, 1, lambda: column(0)),
+        (2, 2, combine_row),
+        (8, 3, lambda: arrive(3, 0)),
+        (4, 4, combine),
+        (16, 4, lambda: column(1)),
+        (4, 8, take_partner),
+        (8, 8, add_prior),
+        (9, 20, lambda: column(2)),
+        (12, 12, normalize),
+        (20, 12, lambda: column(3)),
+        (24, 16, give_back),
+    )
     mine_at, partner_at = y * 4 + x, (3 - y) * 4 + x
 
     def pick(k, values):
         out = values[0]
-        for at in range(1, 8):
+        for at in range(1, len(values)):
             out = jnp.where(k == at, values[at], out)
         return out
 
-    @pl.loop(0, 32)
+    def table(k, column):
+        return jnp.where(low, pick(k, [s[column] for s in LOW]), pick(k, [s[column] for s in HIGH]))
+
+    @pl.loop(0, 25)
     def _(t):
-        for at, act in events.items():
-
-            @pl.when(t == at)
-            def _(act=act):
-                act()
-
-        k = lax.rem(t, 8)
-        far = t // 16
-        g = jnp.where((t >= 8) & (t < 24), 1, 0)
-        a = pick(k, [p[0] for p in NEAR]) + far
-        dx = pick(k, [p[1] for p in NEAR])
+        for at_low, at_high, act in events:
+            pl.when(t == jnp.where(low, at_low, at_high))(act)
+
+        k = lax.rem(t, 4)
+        step = t // 4
+        g, a = table(step, 0), table(step, 1)
+        dx = pick(k, COLUMNS)
         slot = 4 * a + dx
-        row = jnp.where(a == 0, ys[0], jnp.where(a == 1, ys[1], jnp.where(a == 2, ys[2], ys[3])))
+        row = pick(a, ys)
         keys_at = row * 4 + lax.rem(x + dx, 4)
-        asks = jnp.where(g == 0, mine_at, partner_at)
-
-        @pl.when((t < 8) | ((t >= 16) & (t < 24)))
+        asks = jnp.where(t == 24, -1, jnp.where(g == 0, mine_at, partner_at))
+        here = pick(a, [present(p).astype(jnp.int32) for p in range(4)])
+
+        @pl.when((table(step, 2) == 1) & (t < 24) & (here == 1))
         def _():
             prepare(slot)
 
@@ -352,12 +413,6 @@
         def _():
             for r in range(GROUP):
                 tile(g, slot, r, True)
-
-        @pl.when(t == 23)
-        def _():
-            for r in range(GROUP):
-                o_send[r] = result(1, r)
-                o_out(r, half).start()
 
     for r in range(GROUP):
         cols = pl.ds(pl.multiple_of(half * GROUP * HD + r * HD, HD), HD)
@@ -369,17 +424,21 @@
     swap_q.wait_send()
     for a in range(4):
         for dx in range(4):
-            for kind in kinds(a, dx):
-                hop(a, dx, kind).wait_send()
+            for when, kind in onward(a, dx):
+                guarded(when, lambda a=a, dx=dx, kind=kind: hop(a, dx, kind).wait_send())
     for r in range(GROUP):
         o_out(r, half).wait_send()
     for j in range(1, 4):
         energy_out(j).wait_send()
 
-    @pl.loop(1, 32)
+    @pl.loop(1, 8)
     def _(j):
         slice_out(j).wait_send()
         prior_out(j).wait_send()
+
+    @pl.loop(1, 4)
+    def _(j):
+        total_out(j).wait_send()
 
 
 def body(q_lin, k_lin, v_lin, log_decay, lin_gain, q_soft, k_soft, v_soft):
@@ -404,16 +463,19 @@
             pltpu.VMEM((2, TILES, HD), F32),
             pltpu.VMEM((2, TILES, 2 * HD), F32),
             pltpu.VMEM((GROUP, ROWS, HD), F32),
-            pltpu.VMEM((32, 40, HD), F32),
-            pltpu.VMEM((32, 40, HD), F32),
-            pltpu.VMEM((32, 32, HD), F32),
-            pltpu.VMEM((32, 32, HD), F32),
+            pltpu.VMEM((8, HD + 8, HD), F32),
+            pltpu.VMEM((8, HD + 8, HD), F32),
+            pltpu.VMEM((8, HD, HD), F32),
+            pltpu.VMEM((8, 8, HD), F32),
+            pltpu.VMEM((HD + 8, HD), F32),
+            pltpu.VMEM((4, HD + 8, HD), F32),
+            pltpu.VMEM((8, HD, HD), F32),
             pltpu.VMEM((ROWS, HD), F32),
             pltpu.VMEM((3, ROWS, HD), F32),
             pltpu.VMEM((8, ROWS), F32),
             pltpu.VMEM((ROWS, 8), F32),
-            dma((2,)), dma((2,)), dma((16, 4)), dma((16, 3)), dma((GROUP,)), dma((GROUP,)),
-            dma((32,)), dma((32,)), dma((32,)), dma((32,)), dma((3,)), dma((3,)),
+            dma((2,)), dma((2,)), dma((16, 5)), dma((16, 2)), dma((GROUP,)), dma((GROUP,)),
+            dma((8,)), dma((8,)), dma((4,)), dma((4,)), dma((8,)), dma((8,)), dma((3,)), dma((3,)),
         ],
         compiler_params=pltpu.CompilerParams(
             collective_id=0, has_side_effects=True, vmem_limit_bytes=60 << 20

time: 124 us -> 115 us (0.927)
  Pallas kernels: 120 us -> 110 us
    pallas_call x1, Pallas kernels: 120 us -> 110 us  [body(): pl.pallas_call(kernel, out_shape=(jax.ShapeDtypeStruct(q_lin.shape, F32),...]
where the time goes in v2:
time: 115 us; the launch traced here: 114 us
  Pallas kernels  110 us (96%)
  local copies, waits for them, and re-layouts  3.57 us (3%)
    pallas_call x1, Pallas kernels, body(): pl.pallas_call(kernel, out_shape=(jax.ShapeDtypeStruct(q_lin.shape, F32),...  110 us
    unnamed x4, local copies, waits for them, and re-layouts  3.57 us

profile of v2, /device:TPU:30, one launch (start us, length us, event | category | flops | bytes accessed | tf_op | source)
XLA Modules:
  0.0 114.4 jit_solution(12708703891540586323)
XLA Ops:
  0.6 110.2 %attention.1 = (f32[256,1024]{1,0:T(8,128)}, f32[256,1536]{1,0:T(8,128)}) custom-call(f32[256,1024]{1,0:T(8,128)} %q_lin.1, f32[256,1024]{1,0:T(8,128)} %k_lin.1, f32[256,1024]{1,0:T(8,128)} %v_lin.1, f32[8,256]{1,0:T(8,128)} %log_decay.1, f32[1,1024]{1,0:T(1,128)} %bitcast.1, f32[256,1536]{1,0:T(8,128)} %q_soft.1, f32[256,256]{1,0:T(8,128)} %k_soft.1, ...), custom_call_target="tpu_custom_call" | custom-call | flops 6845104128 | bytes 12582912 | tf_op jit(solution)/shard_map/attention/pallas_call | solution.py:447
  110.8 0.0 copy-start
  110.8 2.4 %copy.12 = f32[256,1024]{1,0:T(8,128)} copy(f32[256,1024]{1,0:T(8,128)} %get-tuple-element.4) | data formatting | bytes 2097152
  113.3 0.0 copy-done
  113.3 1.1 copy.13
Async XLA Ops:
  110.8 2.4 %copy-start = (f32[256,1536]{1,0:T(8,128)S(1)}, f32[256,1536]{1,0:T(8,128)}, u32[]{:S(2)}) copy-start(f32[256,1536]{1,0:T(8,128)} %get-tuple-element.5) | copy-start | bytes 4718596

commit v3 on v2

--- a/solution.py
+++ b/solution.py
@@ -21,7 +21,7 @@
 GROUP = 6
 TILES = GROUP * ROWS
 COLUMNS = (0, 3, 1, 2)
-LOW = ((0, 0, 1), (1, 0, 0), (0, 2, 1), (1, 2, 0), (1, 1, 1), (1, 3, 1))
+LOW = ((0, 0, 1), (1, 0, 0), (0, 2, 1), (1, 2, 0), (0, 0, 0), (0, 0, 0))
 HIGH = ((0, 0, 1), (0, 1, 1), (1, 1, 0), (1, 3, 1), (0, 3, 0), (0, 2, 1))
 
 
@@ -43,11 +43,11 @@
 
 
 def kernel(
-    q_lin, k_lin, v_lin, log_decay, gain, q_soft, k_soft, v_soft,
+    q_lin_all, k_lin_all, v_lin_all, log_decay, gain, q_soft, k_soft, v_soft,
     lin_out, soft_out,
-    kv, kv_out, q_in, q3, k3, v2, m_all, l_all, acc, o_send,
+    q_lin, k_lin, v_lin, kv, q_own, q_in, q3, k3, v2, m_all, l_all, acc, o_send,
     local, gathered, prior, reach_decay, row_out, row_in, entering, energy, energy_in, cum_row, cum_col,
-    swap_send, swap_recv, send, recv, o_ss, o_rs, l_ss, l_rs, r_ss, r_rs, e_ss, e_rs, n_ss, n_rs,
+    loaded, swap_send, swap_recv, send, recv, o_ss, o_rs, l_ss, l_rs, r_ss, r_rs, e_ss, e_rs, n_ss, n_rs,
 ):
     me = lax.axis_index("ctx")
     z = lax.axis_index("head")
@@ -94,12 +94,20 @@
 
     for j in range(1, 4):
         pl.semaphore_signal(barrier, inc=1, device_id={"ctx": me, "head": lax.rem(z + j, 4)})
-    mine_col = pl.multiple_of(half * HD, HD)
-    other_col = pl.multiple_of(other * HD, HD)
-    kv[0, core, 0] = k_soft[:, pl.ds(mine_col, HD)]
-    kv[0, core, 1] = v_soft[:, pl.ds(mine_col, HD)]
-    kv_out[0] = k_soft[:, pl.ds(other_col, HD)]
-    kv_out[1] = v_soft[:, pl.ds(other_col, HD)]
+    mine = pl.ds(pl.multiple_of(half * HD, HD), HD)
+    others = pl.ds(pl.multiple_of(other * HD, HD), HD)
+    loads = [
+        pltpu.make_async_copy(k_soft.at[:, mine], kv.at[0, core, 0], loaded.at[0]),
+        pltpu.make_async_copy(v_soft.at[:, mine], kv.at[0, core, 1], loaded.at[1]),
+        pltpu.make_async_copy(q_lin_all, q_lin, loaded.at[2]),
+        pltpu.make_async_copy(k_lin_all, k_lin, loaded.at[3]),
+        pltpu.make_async_copy(v_lin_all, v_lin, loaded.at[4]),
+        pltpu.make_async_copy(
+            q_soft.at[:, pl.ds(pl.multiple_of(half * GROUP * HD, HD), GROUP * HD)], q_own, loaded.at[5]
+        ),
+    ]
+    for load in loads:
+        load.start()
     pl.semaphore_wait(barrier, 13)
 
     def hop(a, dx, kind):
@@ -123,7 +131,8 @@
             out += [(when, 0), (when, 1), (when, 4)]
         return out + [(present(a), 2)]
 
-    swap_kv = remote(kv_out, kv.at[4, core], swap_send.at[0], swap_recv.at[0], partner)
+    swap_k = remote(k_soft.at[:, others], kv.at[4, core, 0], swap_send.at[0], swap_recv.at[0], partner)
+    swap_v = remote(v_soft.at[:, others], kv.at[4, core, 1], swap_send.at[2], swap_recv.at[2], partner)
     q_cols = pl.ds(pl.multiple_of(other * GROUP * HD, HD), GROUP * HD)
     swap_q = remote(q_soft.at[:, q_cols], q_in, swap_send.at[1], swap_recv.at[1], partner)
 
@@ -141,31 +150,34 @@
             remote(part, part, send.at[slot, 0], recv.at[slot, 0], targets[2]).wait_recv()
 
         if (a, dx) == (1, 0):
-            swap_kv.wait_recv()
+            swap_k.wait_recv()
+            swap_v.wait_recv()
         elif (a, dx) != (0, 0):
             guarded(present(a), wait)
         for when, kind in onward(a, dx):
             guarded(when, lambda kind=kind: hop(a, dx, kind).start())
 
-    arrive(0, 0)
-
-    @pl.when(half == 0)
+    @pl.when(low)
     def _():
-        swap_kv.start()
+        swap_k.start()
+        swap_v.start()
         swap_q.start()
 
-    @pl.when(half == 1)
+    @pl.when(high_half)
     def _():
         swap_q.start()
-        swap_kv.start()
+        swap_k.start()
+        swap_v.start()
+
+    loads[0].wait()
+    loads[1].wait()
+    arrive(0, 0)
 
     scale = math.log2(math.e) / math.sqrt(HD)
 
-    def take_queries(g, ref, first):
+    def take_queries(g, ref):
         for r in range(GROUP):
-            col = first + r * HD
-            if not isinstance(col, int):
-                col = pl.multiple_of(col, HD)
+            col = r * HD
             high, low = halves(ref[:, pl.ds(col, HD)] * scale)
             rows = slice(r * ROWS, (r + 1) * ROWS)
             q3[g, rows, :HD] = high
@@ -196,6 +208,8 @@
         local[hd, :HD] = state
         local[hd, HD:] = jnp.broadcast_to(jnp.exp(total), (8, HD))
 
+    for at in (2, 3, 4):
+        loads[at].wait()
     for hd in range(8):
         lightning_head(hd)
 
@@ -212,7 +226,8 @@
         slice_out(j).start()
 
     gathered[at_row] = local[at_row]
-    take_queries(0, q_soft, half * GROUP * HD)
+    loads[5].wait()
+    take_queries(0, q_own)
 
     def total_out(j):
         return remote(row_out, row_in.at[y], r_ss.at[j], r_rs.at[j], device(lax.rem(y + j, 4), x, core))
@@ -317,13 +332,12 @@
                 v2[slot, rows, :HD] = high
                 v2[slot, rows, HD:] = low
 
-    def tile(g, slot, r, masked):
-        rows = slice(r * ROWS, (r + 1) * ROWS)
+    def tile(g, slot, rows, ahead=None):
         scores = lax.dot_general(q3[g, rows, :], k3[slot], NT, preferred_element_type=F32)
-        if masked:
-            at = lax.broadcasted_iota(jnp.int32, (ROWS, KEYS), 0) + core * ROWS
+        if ahead is not None:
+            at = lax.broadcasted_iota(jnp.int32, (ROWS, KEYS), 0)
             key = lax.broadcasted_iota(jnp.int32, (ROWS, KEYS), 1)
-            scores = jnp.where(key <= at, scores, NEGATIVE)
+            scores = jnp.where(key - at <= ahead * KEYS + core * ROWS, scores, NEGATIVE)
         before = m_all[g, rows, :]
         after = jnp.maximum(before, jnp.max(scores, axis=1, keepdims=True))
         weights = jnp.exp2(scores - jnp.concatenate([after] * (KEYS // HD), 1))
@@ -337,8 +351,11 @@
         acc[g, rows, :] = acc[g, rows, :] * jnp.concatenate([shrink, shrink], 1) + summed
         m_all[g, rows, :] = after
 
+    def tile_rows(r):
+        return slice(r * ROWS, (r + 1) * ROWS) if isinstance(r, int) else pl.ds(pl.multiple_of(r * ROWS, ROWS), ROWS)
+
     def result(g, r):
-        rows = slice(r * ROWS, (r + 1) * ROWS)
+        rows = tile_rows(r)
         total = jnp.sum(l_all[g, rows, :], axis=1, keepdims=True)
         return (acc[g, rows, :HD] + acc[g, rows, HD:]) / total
 
@@ -348,7 +365,7 @@
 
     def take_partner():
         swap_q.wait_recv()
-        take_queries(1, q_in, 0)
+        take_queries(1, q_in)
 
     def give_back():
         for r in range(GROUP):
@@ -358,6 +375,37 @@
     def column(a):
         for dx in (3, 1, 2):
             arrive(a, dx)
+
+    mine_at, partner_at = y * 4 + x, (3 - y) * 4 + x
+
+    def finish():
+        column(1)
+        for dx in COLUMNS:
+            prepare(4 + dx)
+        column(3)
+
+        @pl.when(present(3))
+        def _():
+            for dx in COLUMNS:
+                prepare(12 + dx)
+
+        @pl.loop(0, GROUP // 2)
+        def _(pair):
+            both = (2 * pair, 2 * pair + 1)
+            for dx in COLUMNS:
+                keys_at = (3 - y) * 4 + lax.rem(x + dx, 4)
+                for r in both:
+                    tile(1, 4 + dx, tile_rows(r), partner_at - keys_at)
+
+            @pl.when(present(3))
+            def _():
+                for dx in COLUMNS:
+                    for r in both:
+                        tile(1, 12 + dx, tile_rows(r))
+
+            for r in both:
+                o_send[r] = result(1, r)
+                o_out(r, half).start()
 
     events = (
         (0, 10, lambda: arrive(2, 0)),
@@ -365,17 +413,16 @@
         (1, 1, lambda: column(0)),
         (2, 2, combine_row),
         (8, 3, lambda: arrive(3, 0)),
-        (4, 4, combine),
-        (16, 4, lambda: column(1)),
+        (99, 4, lambda: column(1)),
         (4, 8, take_partner),
-        (8, 8, add_prior),
+        (8, 6, combine),
         (9, 20, lambda: column(2)),
-        (12, 12, normalize),
-        (20, 12, lambda: column(3)),
-        (24, 16, give_back),
+        (12, 14, add_prior),
+        (99, 12, lambda: column(3)),
+        (15, 20, normalize),
+        (99, 16, give_back),
+        (16, 99, finish),
     )
-    mine_at, partner_at = y * 4 + x, (3 - y) * 4 + x
-
     def pick(k, values):
         out = values[0]
         for at in range(1, len(values)):
@@ -385,7 +432,7 @@
     def table(k, column):
         return jnp.where(low, pick(k, [s[column] for s in LOW]), pick(k, [s[column] for s in HIGH]))
 
-    @pl.loop(0, 25)
+    @pl.loop(0, 24)
     def _(t):
         for at_low, at_high, act in events:
             pl.when(t == jnp.where(low, at_low, at_high))(act)
@@ -397,22 +444,22 @@
         slot = 4 * a + dx
         row = pick(a, ys)
         keys_at = row * 4 + lax.rem(x + dx, 4)
-        asks = jnp.where(t == 24, -1, jnp.where(g == 0, mine_at, partner_at))
+        asks = jnp.where(low & (t >= 16), -1, jnp.where(g == 0, mine_at, partner_at))
         here = pick(a, [present(p).astype(jnp.int32) for p in range(4)])
 
-        @pl.when((table(step, 2) == 1) & (t < 24) & (here == 1))
+        @pl.when((table(step, 2) == 1) & (here == 1))
         def _():
             prepare(slot)
 
         @pl.when(keys_at < asks)
         def _():
             for r in range(GROUP):
-                tile(g, slot, r, False)
+                tile(g, slot, tile_rows(r))
 
         @pl.when(keys_at == asks)
         def _():
             for r in range(GROUP):
-                tile(g, slot, r, True)
+                tile(g, slot, tile_rows(r), 0)
 
     for r in range(GROUP):
         cols = pl.ds(pl.multiple_of(half * GROUP * HD + r * HD, HD), HD)
@@ -420,7 +467,8 @@
     for r in range(GROUP):
         o_out(r, other).wait_recv()
 
-    swap_kv.wait_send()
+    swap_k.wait_send()
+    swap_v.wait_send()
     swap_q.wait_send()
     for a in range(4):
         for dx in range(4):
@@ -443,6 +491,7 @@
 
 def body(q_lin, k_lin, v_lin, log_decay, lin_gain, q_soft, k_soft, v_soft):
     vmem = pl.BlockSpec(memory_space=pltpu.VMEM)
+    hbm = pl.BlockSpec(memory_space=pl.ANY)
     dma = pltpu.SemaphoreType.DMA
     return pl.pallas_call(
         kernel,
@@ -450,11 +499,14 @@
             jax.ShapeDtypeStruct(q_lin.shape, F32),
             jax.ShapeDtypeStruct(q_soft.shape, F32),
         ),
-        in_specs=[vmem] * 8,
+        in_specs=[hbm] * 3 + [vmem] * 2 + [hbm] * 3,
         out_specs=(vmem, vmem),
         scratch_shapes=[
+            pltpu.VMEM((ROWS, 8 * HD), F32),
+            pltpu.VMEM((ROWS, 8 * HD), F32),
+            pltpu.VMEM((ROWS, 8 * HD), F32),
             pltpu.VMEM((16, 2, 2, ROWS, HD), F32),
-            pltpu.VMEM((2, ROWS, HD), F32),
+            pltpu.VMEM((ROWS, GROUP * HD), F32),
             pltpu.VMEM((ROWS, GROUP * HD), F32),
             pltpu.VMEM((2, TILES, 3 * HD), BF16),
             pltpu.VMEM((16, KEYS, 3 * HD), BF16),
@@ -474,7 +526,7 @@
             pltpu.VMEM((3, ROWS, HD), F32),
             pltpu.VMEM((8, ROWS), F32),
             pltpu.VMEM((ROWS, 8), F32),
-            dma((2,)), dma((2,)), dma((16, 5)), dma((16, 2)), dma((GROUP,)), dma((GROUP,)),
+            dma((6,)), dma((3,)), dma((3,)), dma((16, 5)), dma((16, 2)), dma((GROUP,)), dma((GROUP,)),
             dma((8,)), dma((8,)), dma((4,)), dma((4,)), dma((8,)), dma((8,)), dma((3,)), dma((3,)),
         ],
         compiler_params=pltpu.CompilerParams(

time: 115 us -> 114 us (level)
  the two profiles are of different devices: /device:TPU:30 before, /device:TPU:1 now
where the time goes in v3:
time: 114 us
  Pallas kernels  110 us (96%)
  local copies, waits for them, and re-layouts  3.57 us (3%)
    pallas_call x1, Pallas kernels, body(): pl.pallas_call(kernel, out_shape=(jax.ShapeDtypeStruct(q_lin.shape, F32),...  110 us
    unnamed x4, local copies, waits for them, and re-layouts  3.57 us

profile of v3, /device:TPU:1, one launch (start us, length us, event | category | flops | bytes accessed | tf_op | source)
XLA Modules:
  0.0 113.9 jit_solution(6433955061464609693)
XLA Ops:
  0.6 109.6 %attention.1 = (f32[256,1024]{1,0:T(8,128)}, f32[256,1536]{1,0:T(8,128)}) custom-call(f32[256,1024]{1,0:T(8,128)} %q_lin_all.1, f32[256,1024]{1,0:T(8,128)} %k_lin_all.1, f32[256,1024]{1,0:T(8,128)} %v_lin_all.1, f32[8,256]{1,0:T(8,128)} %log_decay.1, f32[1,1024]{1,0:T(1,128)} %bitcast.1, f32[256,1536]{1,0:T(8,128)} %q_soft.1, f32[256,256]{1,0:T(8,128)} %k_soft.1, ...), custom_call_target="tpu_custom_call" | custom-call | flops 6845104128 | bytes 12582912 | tf_op jit(solution)/shard_map/attention/pallas_call | solution.py:496
  110.3 0.0 copy-start
  110.3 2.4 %copy.12 = f32[256,1024]{1,0:T(8,128)} copy(f32[256,1024]{1,0:T(8,128)} %get-tuple-element.4) | data formatting | bytes 2097152
  112.7 0.0 copy-done
  112.7 1.1 %copy.13 = f32[256,1536]{1,0:T(8,128)} copy(f32[256,1536]{1,0:T(8,128)S(1)} %copy-done) | data formatting | bytes 3145728
Async XLA Ops:
  110.3 2.4 %copy-start = (f32[256,1536]{1,0:T(8,128)S(1)}, f32[256,1536]{1,0:T(8,128)}, u32[]{:S(2)}) copy-start(f32[256,1536]{1,0:T(8,128)} %get-tuple-element.5) | copy-start | bytes 4718596

commit v4 on v3

--- a/solution.py
+++ b/solution.py
@@ -157,18 +157,9 @@
         for when, kind in onward(a, dx):
             guarded(when, lambda kind=kind: hop(a, dx, kind).start())
 
-    @pl.when(low)
-    def _():
-        swap_k.start()
-        swap_v.start()
-        swap_q.start()
-
-    @pl.when(high_half)
-    def _():
-        swap_q.start()
-        swap_k.start()
-        swap_v.start()
-
+    swap_k.start()
+    swap_v.start()
+    swap_q.start()
     loads[0].wait()
     loads[1].wait()
     arrive(0, 0)
@@ -391,6 +382,7 @@
 
         @pl.loop(0, GROUP // 2)
         def _(pair):
+            pl.when(pair == 1)(add_prior)
             both = (2 * pair, 2 * pair + 1)
             for dx in COLUMNS:
                 keys_at = (3 - y) * 4 + lax.rem(x + dx, 4)
@@ -409,20 +401,20 @@
 
     events = (
         (0, 10, lambda: arrive(2, 0)),
-        (6, 0, lambda: arrive(1, 0)),
+        (1, 0, lambda: arrive(1, 0)),
         (1, 1, lambda: column(0)),
-        (2, 2, combine_row),
-        (8, 3, lambda: arrive(3, 0)),
+        (2, 3, lambda: arrive(3, 0)),
         (99, 4, lambda: column(1)),
         (4, 8, take_partner),
-        (8, 6, combine),
+        (4, 5, combine_row),
         (9, 20, lambda: column(2)),
-        (12, 14, add_prior),
+        (12, 12, combine),
         (99, 12, lambda: column(3)),
-        (15, 20, normalize),
+        (99, 17, add_prior),
         (99, 16, give_back),
         (16, 99, finish),
     )
+
     def pick(k, values):
         out = values[0]
         for at in range(1, len(values)):
@@ -461,6 +453,7 @@
             for r in range(GROUP):
                 tile(g, slot, tile_rows(r), 0)
 
+    normalize()
     for r in range(GROUP):
         cols = pl.ds(pl.multiple_of(half * GROUP * HD + r * HD, HD), HD)
         soft_out[:, cols] = result(0, r)

time: 114 us -> 93.5 us (0.82)
  the two profiles are of different devices: /device:TPU:1 before, /device:TPU:14 now
where the time goes in v4:
time: 93.5 us; the launch traced here: 93.3 us
  Pallas kernels  89.1 us (95%)
  local copies, waits for them, and re-layouts  3.57 us (4%)
    pallas_call x1, Pallas kernels, body(): pl.pallas_call(kernel, out_shape=(jax.ShapeDtypeStruct(q_lin.shape, F32),...  89.1 us
    unnamed x4, local copies, waits for them, and re-layouts  3.57 us

profile of v4, /device:TPU:14, one launch (start us, length us, event | category | flops | bytes accessed | tf_op | source)
XLA Modules:
  0.0 93.3 jit_solution(5405325634282117878)
XLA Ops:
  0.6 89.1 %attention.1 = (f32[256,1024]{1,0:T(8,128)}, f32[256,1536]{1,0:T(8,128)}) custom-call(f32[256,1024]{1,0:T(8,128)} %q_lin_all.1, f32[256,1024]{1,0:T(8,128)} %k_lin_all.1, f32[256,1024]{1,0:T(8,128)} %v_lin_all.1, f32[8,256]{1,0:T(8,128)} %log_decay.1, f32[1,1024]{1,0:T(1,128)} %bitcast.1, f32[256,1536]{1,0:T(8,128)} %q_soft.1, f32[256,256]{1,0:T(8,128)} %k_soft.1, ...), custom_call_target="tpu_custom_call" | custom-call | flops 6845104128 | bytes 12582912 | tf_op jit(solution)/shard_map/attention/pallas_call | solution.py:489
  89.8 0.0 copy-start
  89.8 2.4 %copy.12 = f32[256,1024]{1,0:T(8,128)} copy(f32[256,1024]{1,0:T(8,128)} %get-tuple-element.4) | data formatting | bytes 2097152
  92.2 0.0 copy-done
  92.2 1.1 %copy.13 = f32[256,1536]{1,0:T(8,128)} copy(f32[256,1536]{1,0:T(8,128)S(1)} %copy-done) | data formatting | bytes 3145728
Async XLA Ops:
  89.8 2.4 %copy-start = (f32[256,1536]{1,0:T(8,128)S(1)}, f32[256,1536]{1,0:T(8,128)}, u32[]{:S(2)}) copy-start(f32[256,1536]{1,0:T(8,128)} %get-tuple-element.5) | copy-start | bytes 4718596

commit v5 on v4

--- a/solution.py
+++ b/solution.py
@@ -21,8 +21,11 @@
 GROUP = 6
 TILES = GROUP * ROWS
 COLUMNS = (0, 3, 1, 2)
-LOW = ((0, 0, 1), (1, 0, 0), (0, 2, 1), (1, 2, 0), (0, 0, 0), (0, 0, 0))
-HIGH = ((0, 0, 1), (0, 1, 1), (1, 1, 0), (1, 3, 1), (0, 3, 0), (0, 2, 1))
+SETS = (
+    ((0, 0, 1), (1, 0, 0), (0, 2, 1), (0, 0, 0), (0, 0, 0), (0, 0, 0)),
+    ((0, 0, 1), (1, 0, 0), (1, 1, 1), (0, 0, 0), (0, 0, 0), (0, 0, 0)),
+    ((0, 0, 1), (0, 1, 1), (1, 1, 0), (1, 3, 1), (0, 3, 0), (0, 2, 1)),
+)
 
 
 def halves(value):
@@ -123,11 +126,11 @@
     def onward(a, dx):
         out = []
         if a < 2:
-            out.append((inner | (low, high_half)[a] if dx == 0 else inner, 3))
+            out.append((inner | (low, high_half)[a] if dx == 0 else inner | low, 3))
             if a == 1 and dx != 0:
                 out = []
-        if dx == 0:
-            when = (always, always, inner & low, present(3))[a]
+        if dx == 0 and a != 2:
+            when = present(a)
             out += [(when, 0), (when, 1), (when, 4)]
         return out + [(present(a), 2)]
 
@@ -369,50 +372,60 @@
 
     mine_at, partner_at = y * 4 + x, (3 - y) * 4 + x
 
+    def by_kind(values):
+        return jnp.where(low, jnp.where(inner, values[0], values[1]), values[2])
+
+    outer = jnp.logical_not(inner)
+    end_a = jnp.where(inner, 1, 3)
+    end_row = jnp.where(inner, ys[1], ys[3])
+
     def finish():
-        column(1)
-        for dx in COLUMNS:
-            prepare(4 + dx)
-        column(3)
-
-        @pl.when(present(3))
+        @pl.when(inner)
         def _():
+            column(1)
+            for dx in COLUMNS:
+                prepare(4 + dx)
+
+        @pl.when(outer)
+        def _():
+            column(3)
             for dx in COLUMNS:
                 prepare(12 + dx)
+            column(2)
+            for dx in COLUMNS:
+                prepare(8 + dx)
 
         @pl.loop(0, GROUP // 2)
         def _(pair):
             pl.when(pair == 1)(add_prior)
             both = (2 * pair, 2 * pair + 1)
             for dx in COLUMNS:
-                keys_at = (3 - y) * 4 + lax.rem(x + dx, 4)
+                keys_at = end_row * 4 + lax.rem(x + dx, 4)
                 for r in both:
-                    tile(1, 4 + dx, tile_rows(r), partner_at - keys_at)
-
-            @pl.when(present(3))
-            def _():
-                for dx in COLUMNS:
-                    for r in both:
-                        tile(1, 12 + dx, tile_rows(r))
+                    tile(1, 4 * end_a + dx, tile_rows(r), partner_at - keys_at)
+
+            for dx in COLUMNS:
+                for r in both:
+                    tile(1, 8 + dx, tile_rows(r))
 
             for r in both:
                 o_send[r] = result(1, r)
                 o_out(r, half).start()
 
     events = (
-        (0, 10, lambda: arrive(2, 0)),
-        (1, 0, lambda: arrive(1, 0)),
-        (1, 1, lambda: column(0)),
-        (2, 3, lambda: arrive(3, 0)),
-        (99, 4, lambda: column(1)),
-        (4, 8, take_partner),
-        (4, 5, combine_row),
-        (9, 20, lambda: column(2)),
-        (12, 12, combine),
-        (99, 12, lambda: column(3)),
-        (99, 17, add_prior),
-        (99, 16, give_back),
-        (16, 99, finish),
+        ((0, 0, 10), lambda: arrive(2, 0)),
+        ((1, 1, 0), lambda: arrive(1, 0)),
+        ((1, 1, 1), lambda: column(0)),
+        ((2, 2, 3), lambda: arrive(3, 0)),
+        ((99, 8, 4), lambda: column(1)),
+        ((4, 4, 8), take_partner),
+        ((4, 4, 5), combine_row),
+        ((8, 99, 20), lambda: column(2)),
+        ((11, 10, 12), combine),
+        ((99, 99, 12), lambda: column(3)),
+        ((99, 99, 17), add_prior),
+        ((99, 99, 16), give_back),
+        ((12, 12, 99), finish),
     )
 
     def pick(k, values):
@@ -422,12 +435,12 @@
         return out
 
     def table(k, column):
-        return jnp.where(low, pick(k, [s[column] for s in LOW]), pick(k, [s[column] for s in HIGH]))
+        return by_kind([pick(k, [s[column] for s in sets]) for sets in SETS])
 
     @pl.loop(0, 24)
     def _(t):
-        for at_low, at_high, act in events:
-            pl.when(t == jnp.where(low, at_low, at_high))(act)
+        for at, act in events:
+            pl.when(t == by_kind(at))(act)
 
         k = lax.rem(t, 4)
         step = t // 4
@@ -436,7 +449,7 @@
         slot = 4 * a + dx
         row = pick(a, ys)
         keys_at = row * 4 + lax.rem(x + dx, 4)
-        asks = jnp.where(low & (t >= 16), -1, jnp.where(g == 0, mine_at, partner_at))
+        asks = jnp.where(low & (t >= 12), -1, jnp.where(g == 0, mine_at, partner_at))
         here = pick(a, [present(p).astype(jnp.int32) for p in range(4)])
 
         @pl.when((table(step, 2) == 1) & (here == 1))

time: 93.5 us -> 93.4 us (level)
  no operation moved by 1% of the time
where the time goes in v5:
time: 93.4 us; the launch traced here: 93.2 us
  Pallas kernels  89 us (95%)
  local copies, waits for them, and re-layouts  3.57 us (4%)
    pallas_call x1, Pallas kernels, body(): pl.pallas_call(kernel, out_shape=(jax.ShapeDtypeStruct(q_lin.shape, F32),...  89 us
    unnamed x4, local copies, waits for them, and re-layouts  3.57 us

profile of v5, /device:TPU:14, one launch (start us, length us, event | category | flops | bytes accessed | tf_op | source)
XLA Modules:
  0.0 93.2 jit_solution(17524773581963300828)
XLA Ops:
  0.6 89.0 %attention.1 = (f32[256,1024]{1,0:T(8,128)}, f32[256,1536]{1,0:T(8,128)}) custom-call(f32[256,1024]{1,0:T(8,128)} %q_lin_all.1, f32[256,1024]{1,0:T(8,128)} %k_lin_all.1, f32[256,1024]{1,0:T(8,128)} %v_lin_all.1, f32[8,256]{1,0:T(8,128)} %log_decay.1, f32[1,1024]{1,0:T(1,128)} %bitcast.1, f32[256,1536]{1,0:T(8,128)} %q_soft.1, f32[256,256]{1,0:T(8,128)} %k_soft.1, ...), custom_call_target="tpu_custom_call" | custom-call | flops 6845104128 | bytes 12582912 | tf_op jit(solution)/shard_map/attention/pallas_call | solution.py:502
  89.7 0.0 copy-start
  89.7 2.4 %copy.12 = f32[256,1024]{1,0:T(8,128)} copy(f32[256,1024]{1,0:T(8,128)} %get-tuple-element.4) | data formatting | bytes 2097152
  92.1 0.0 copy-done
  92.1 1.1 %copy.13 = f32[256,1536]{1,0:T(8,128)} copy(f32[256,1536]{1,0:T(8,128)S(1)} %copy-done) | data formatting | bytes 3145728
Async XLA Ops:
  89.7 2.4 %copy-start = (f32[256,1536]{1,0:T(8,128)S(1)}, f32[256,1536]{1,0:T(8,128)}, u32[]{:S(2)}) copy-start(f32[256,1536]{1,0:T(8,128)} %get-tuple-element.5) | copy-start | bytes 4718596

commit v6 on v5

--- a/solution.py
+++ b/solution.py
@@ -24,7 +24,7 @@
 SETS = (
     ((0, 0, 1), (1, 0, 0), (0, 2, 1), (0, 0, 0), (0, 0, 0), (0, 0, 0)),
     ((0, 0, 1), (1, 0, 0), (1, 1, 1), (0, 0, 0), (0, 0, 0), (0, 0, 0)),
-    ((0, 0, 1), (0, 1, 1), (1, 1, 0), (1, 3, 1), (0, 3, 0), (0, 2, 1)),
+    ((0, 0, 1), (1, 1, 1), (1, 3, 1), (0, 1, 0), (0, 3, 0), (0, 2, 1)),
 )
 
 
@@ -418,13 +418,13 @@
         ((1, 1, 1), lambda: column(0)),
         ((2, 2, 3), lambda: arrive(3, 0)),
         ((99, 8, 4), lambda: column(1)),
-        ((4, 4, 8), take_partner),
+        ((4, 4, 4), take_partner),
         ((4, 4, 5), combine_row),
         ((8, 99, 20), lambda: column(2)),
         ((11, 10, 12), combine),
-        ((99, 99, 12), lambda: column(3)),
+        ((99, 99, 8), lambda: column(3)),
         ((99, 99, 17), add_prior),
-        ((99, 99, 16), give_back),
+        ((99, 99, 12), give_back),
         ((12, 12, 99), finish),
     )
 

time: 93.4 us -> 89.6 us (0.959)
  the two profiles are of different devices: /device:TPU:14 before, /device:TPU:30 now
where the time goes in v6:
time: 89.6 us; the launch traced here: 88.2 us
  Pallas kernels  83.9 us (94%)
  local copies, waits for them, and re-layouts  3.57 us (4%)
    pallas_call x1, Pallas kernels, body(): pl.pallas_call(kernel, out_shape=(jax.ShapeDtypeStruct(q_lin.shape, F32),...  83.9 us
    unnamed x4, local copies, waits for them, and re-layouts  3.57 us

profile of v6, /device:TPU:30, one launch (start us, length us, event | category | flops | bytes accessed | tf_op | source)
XLA Modules:
  0.0 88.2 jit_solution(7870593597302825459)
XLA Ops:
  0.6 83.9 %attention.1 = (f32[256,1024]{1,0:T(8,128)}, f32[256,1536]{1,0:T(8,128)}) custom-call(f32[256,1024]{1,0:T(8,128)} %q_lin_all.1, f32[256,1024]{1,0:T(8,128)} %k_lin_all.1, f32[256,1024]{1,0:T(8,128)} %v_lin_all.1, f32[8,256]{1,0:T(8,128)} %log_decay.1, f32[1,1024]{1,0:T(1,128)} %bitcast.1, f32[256,1536]{1,0:T(8,128)} %q_soft.1, f32[256,256]{1,0:T(8,128)} %k_soft.1, ...), custom_call_target="tpu_custom_call" | custom-call | flops 6845104128 | bytes 12582912 | tf_op jit(solution)/shard_map/attention/pallas_call | solution.py:502
  84.6 0.0 copy-start
  84.6 2.4 %copy.12 = f32[256,1024]{1,0:T(8,128)} copy(f32[256,1024]{1,0:T(8,128)} %get-tuple-element.4) | data formatting | bytes 2097152
  87.0 0.0 copy-done
  87.0 1.1 %copy.13 = f32[256,1536]{1,0:T(8,128)} copy(f32[256,1536]{1,0:T(8,128)S(1)} %copy-done) | data formatting | bytes 3145728
Async XLA Ops:
  84.6 2.4 %copy-start = (f32[256,1536]{1,0:T(8,128)S(1)}, f32[256,1536]{1,0:T(8,128)}, u32[]{:S(2)}) copy-start(f32[256,1536]{1,0:T(8,128)} %get-tuple-element.5) | copy-start | bytes 4718596

commit v7 on v6

--- a/solution.py
+++ b/solution.py
@@ -23,8 +23,8 @@
 COLUMNS = (0, 3, 1, 2)
 SETS = (
     ((0, 0, 1), (1, 0, 0), (0, 2, 1), (0, 0, 0), (0, 0, 0), (0, 0, 0)),
-    ((0, 0, 1), (1, 0, 0), (1, 1, 1), (0, 0, 0), (0, 0, 0), (0, 0, 0)),
-    ((0, 0, 1), (1, 1, 1), (1, 3, 1), (0, 1, 0), (0, 3, 0), (0, 2, 1)),
+    ((0, 0, 1), (1, 0, 0), (1, 1, 0), (0, 0, 0), (0, 0, 0), (0, 0, 0)),
+    ((0, 0, 1), (1, 1, 0), (1, 3, 1), (0, 1, 0), (0, 3, 0), (0, 2, 1)),
 )
 
 
@@ -379,13 +379,12 @@
     end_a = jnp.where(inner, 1, 3)
     end_row = jnp.where(inner, ys[1], ys[3])
 
+    def take_row():
+        column(1)
+        for dx in COLUMNS:
+            prepare(4 + dx)
+
     def finish():
-        @pl.when(inner)
-        def _():
-            column(1)
-            for dx in COLUMNS:
-                prepare(4 + dx)
-
         @pl.when(outer)
         def _():
             column(3)
@@ -417,9 +416,9 @@
         ((1, 1, 0), lambda: arrive(1, 0)),
         ((1, 1, 1), lambda: column(0)),
         ((2, 2, 3), lambda: arrive(3, 0)),
-        ((99, 8, 4), lambda: column(1)),
+        ((4, 4, 4), take_row),
+        ((4, 4, 4), combine_row),
         ((4, 4, 4), take_partner),
-        ((4, 4, 5), combine_row),
         ((8, 99, 20), lambda: column(2)),
         ((11, 10, 12), combine),
         ((99, 99, 8), lambda: column(3)),

time: 89.6 us -> 92.8 us (1.036)
  Pallas kernels: 83.9 us -> 88 us
    pallas_call x1, Pallas kernels: 83.9 us -> 88 us  [body(): pl.pallas_call(kernel, out_shape=(jax.ShapeDtypeStruct(q_lin.shape, F32),...]
where the time goes in v7:
time: 92.8 us; the launch traced here: 92.2 us
  Pallas kernels  88 us (95%)
  local copies, waits for them, and re-layouts  3.57 us (4%)
    pallas_call x1, Pallas kernels, body(): pl.pallas_call(kernel, out_shape=(jax.ShapeDtypeStruct(q_lin.shape, F32),...  88 us
    unnamed x4, local copies, waits for them, and re-layouts  3.57 us

profile of v7, /device:TPU:30, one launch (start us, length us, event | category | flops | bytes accessed | tf_op | source)
XLA Modules:
  0.0 92.2 jit_solution(16653860198383893633)
XLA Ops:
  0.6 88.0 %attention.1 = (f32[256,1024]{1,0:T(8,128)}, f32[256,1536]{1,0:T(8,128)}) custom-call(f32[256,1024]{1,0:T(8,128)} %q_lin_all.1, f32[256,1024]{1,0:T(8,128)} %k_lin_all.1, f32[256,1024]{1,0:T(8,128)} %v_lin_all.1, f32[8,256]{1,0:T(8,128)} %log_decay.1, f32[1,1024]{1,0:T(1,128)} %bitcast.1, f32[256,1536]{1,0:T(8,128)} %q_soft.1, f32[256,256]{1,0:T(8,128)} %k_soft.1, ...), custom_call_target="tpu_custom_call" | custom-call | flops 6845104128 | bytes 12582912 | tf_op jit(solution)/shard_map/attention/pallas_call | solution.py:501
  88.6 0.0 copy-start
  88.6 2.4 %copy.12 = f32[256,1024]{1,0:T(8,128)} copy(f32[256,1024]{1,0:T(8,128)} %get-tuple-element.4) | data formatting | bytes 2097152
  91.1 0.0 copy-done
  91.1 1.1 %copy.13 = f32[256,1536]{1,0:T(8,128)} copy(f32[256,1536]{1,0:T(8,128)S(1)} %copy-done) | data formatting | bytes 3145728
Async XLA Ops:
  88.6 2.4 %copy-start = (f32[256,1536]{1,0:T(8,128)S(1)}, f32[256,1536]{1,0:T(8,128)}, u32[]{:S(2)}) copy-start(f32[256,1536]{1,0:T(8,128)} %get-tuple-element.5) | copy-start | bytes 4718596
